TPU v7x, 32 devices: a whole 2x2x4 slice. The times are simulated.
32 devices in a mesh: lag: 16 (over z, x, core), pts: 2 (over y).
Axes of the slice: x: 2, y: 2, z: 4, core: 2. Of those that a mesh axis runs over, the one named last changes fastest.
Arguments:
- history: bfloat16 [96, 512, 128], P('lag'), may hold values from -6 to 6
- incident: bfloat16 [4, 512, 128], P(None, 'pts'), may hold values from -6 to 6
- kernel_blocks: bfloat16 [6144, 128, 128], P(('lag', 'pts')), may hold values from -0.013671875 to 0.013671875
- block_row: int32 [6144], P(('lag', 'pts')), may hold values from 0 to 1
- block_col: int32 [6144], P(('lag', 'pts')), may hold values from 0 to 3
- lag_offset: int32 [6144], P(('lag', 'pts')), may hold values from 0 to 5
- mode_kernel: float32 [96, 128], P('lag'), may hold values from 0.25 to 2
- self_inverse: float32 [512, 128], P('pts'), as said below
Outputs:
- densities: float32 [4, 512, 128], P(None, 'pts')
Inputs may be any that keep to these rules, and one draw needn't show every extreme that they name: Each point block of self_inverse is the identity plus independent entries.
All inputs are finite; a program needn't handle non-finite values.
Results may differ from a plain program's by a relative error of at most 0.00031.
Values may be sent and summed in bfloat16 or wider, within the bound.
A program may use at most 128 MiB of HBM per device.

v0:
```python
import jax
import jax.numpy as jnp
from jax import lax
from jax.sharding import PartitionSpec as P

STEPS = 4


def from_behind(block, axis, distance):
    devices = range(lax.axis_size(axis))
    route = [(i - distance, i) for i in devices if i - distance in devices]
    return lax.ppermute(block, axis, route)


def apply_inverse(inverse_blocks, net_field):
    row_blocks = inverse_blocks.shape[0]
    block_size = inverse_blocks.shape[1]
    shaped = net_field.reshape(row_blocks, block_size, net_field.shape[1])
    solved = jnp.einsum("rij,rjm->rim", inverse_blocks, shaped, precision=lax.Precision.HIGHEST)
    return solved.reshape(net_field.shape[0], net_field.shape[1])


def per_device(
    history, incident, kernel_blocks, block_row, block_col, lag_offset, mode_kernel, self_inverse
):
    lags_held = history.shape[0]
    all_points = history.shape[1]
    mode_cols = history.shape[2]
    entries = kernel_blocks.shape[0]
    block_size = kernel_blocks.shape[1]
    rows_here = self_inverse.shape[0]
    row_blocks = rows_here // block_size
    col_blocks = all_points // block_size
    pair_index = block_row * lags_held + lag_offset
    selector = (
        pair_index[None, :] == jnp.arange(row_blocks * lags_held, dtype=jnp.int32)[:, None]
    ).astype(jnp.float32)
    inverse_blocks = self_inverse.reshape(row_blocks, block_size, block_size)
    first_lag = lax.axis_index("lag") == 0
    held_slabs = history
    densities = []
    for instant in range(STEPS):
        by_block = held_slabs.reshape(lags_held, col_blocks, block_size, mode_cols)
        picked = by_block[lag_offset, block_col]
        products = jnp.einsum(
            "eij,ejm->eim", kernel_blocks, picked, preferred_element_type=jnp.float32
        )
        grouped = jnp.dot(
            selector,
            products.reshape(entries, block_size * mode_cols),
            precision=lax.Precision.HIGHEST,
        )
        grouped = (
            grouped.reshape(row_blocks, lags_held, block_size, mode_cols)
            * mode_kernel[None, :, None, :]
        )
        partial_field = jnp.sum(grouped, axis=1).reshape(rows_here, mode_cols)
        driving = incident[instant].astype(jnp.float32)
        field_share = lax.psum_scatter(partial_field, "lag", scatter_dimension=1, tiled=True)
        share_cols = field_share.shape[1]
        first_col = lax.axis_index("lag") * share_cols
        net_share = lax.dynamic_slice_in_dim(driving, first_col, share_cols, 1) - field_share
        density = lax.all_gather(
            apply_inverse(inverse_blocks, net_share), "lag", axis=1, tiled=True
        )
        densities.append(density)
        if instant + 1 < STEPS:
            new_slab = density.astype(jnp.bfloat16)
            gathered = lax.all_gather(new_slab, "pts", axis=0, tiled=True)
            arrived = from_behind(held_slabs[lags_held - 1], "lag", 1)
            entering = jnp.where(first_lag, gathered, arrived)
            held_slabs = jnp.concatenate([entering[None], held_slabs[: lags_held - 1]], axis=0)
    return jnp.stack(densities)


def solution(mesh):
    return jax.shard_map(
        per_device,
        mesh=mesh,
        in_specs=(
            P("lag", None, None),
            P(None, "pts", None),
            P(("lag", "pts"), None, None),
            P(("lag", "pts")),
            P(("lag", "pts")),
            P(("lag", "pts")),
            P("lag", None),
            P("pts", None),
        ),
        out_specs=P(None, "pts", None),
        check_vma=False,
    )
```

profile of v0, /device:TPU:1, one launch (start us, length us, event | category | flops | bytes accessed | tf_op | source)
XLA Modules:
  0.0 551.6 jit_solution(4356175561156982711)
XLA Ops:
  18.7 10.6 %gather_fusion = bf16[192,128,128]{2,1,0:T(8,128)(2,1)} fusion(bf16[6,4,128,128]{3,2,1,0:T(8,128)(2,1)} %bitcast.200, s32[192]{0:T(256)S(1)} %get-tuple-element.13), kind=kCustom, calls=%fused_computation | custom fusion | bytes 12584448 | tf_op jit(solution)/shard_map/gather | solution.py:44
  29.3 13.7 %convolution_bitcast_fusion.3 = f32[192,128,128]{1,2,0:T(8,128)} fusion(bf16[192,128,128]{2,1,0:T(8,128)(2,1)} %gather_fusion, bf16[192,128,128]{2,1,0:T(8,128)(2,1)} %param.10), kind=kOutput, calls=%fused_computation.23 | convolution fusion | flops 805306368 | bytes 25165824 | tf_op jit(solution)/shard_map/eij,ejm->eim/dot_general | solution.py:45
  43.0 12.6 %copy.36 = f32[192,128,128]{2,1,0:T(8,128)} copy(f32[192,128,128]{1,2,0:T(8,128)} %convolution_bitcast_fusion.3) | data formatting | bytes 25165824 | tf_op jit(solution)/shard_map/eij,ejm->eim/dot_general | solution.py:45
  55.6 16.2 %fusion.15 = f32[2,128,128]{2,1,0:T(8,128)S(1)} fusion(f32[6,128]{1,0:T(8,128)S(1)} %copy-done.3, s32[2,6]{1,0:T(2,128)S(1)} %multiply_add_fusion, s32[192]{0:T(256)S(1)} %get-tuple-element.12, f32[24,8,128,128]{3,2,1,0:T(8,128)} %bitcast.202), kind=kOutput, calls=%fused_computation.31 | convolution fusion | flops 453347584 | bytes 12717872 | tf_op jit(solution)/shard_map/dot_general | solution.py:48
  73.0 52.7 %reduce-scatter.5.cloned.1.call-done = f32[256,8]{0,1:T(8,128)} async-done(((f32[256,128]{0,1:T(8,128)}), f32[256,8]{0,1:T(8,128)}) %reduce-scatter.5.cloned.1.call-update) | async-done | bytes 8208 | tf_op jit(solution)/shard_map/reduce_scatter | solution.py:59
  126.7 22.2 %all_gather.21 = f32[256,128]{0,1:T(8,128)S(1)} all-gather(f32[256,8]{0,1:T(8,128)S(1)} %convolution_bitcast_fusion.7), channel_id=1, replica_groups=mesh['lag'=16,'pts'=2] {'lag'}, dimensions={1}, use_global_device_ids=true | all-gather | bytes 139264 | tf_op jit(solution)/shard_map/all_gather | solution.py:63
  153.4 9.7 %gather_fusion.1 = bf16[192,128,128]{2,1,0:T(8,128)(2,1)} fusion(bf16[6,4,128,128]{3,2,1,0:T(8,128)(2,1)S(1)} %pad_maximum_fusion, s32[192]{0:T(256)S(1)} %get-tuple-element.13), kind=kCustom, calls=%fused_computation.1 | custom fusion | bytes 12584448 | tf_op jit(solution)/shard_map/gather | solution.py:44
  163.1 13.7 %convolution_bitcast_fusion.2 = f32[192,128,128]{1,2,0:T(8,128)} fusion(bf16[192,128,128]{2,1,0:T(8,128)(2,1)} %gather_fusion.1, bf16[192,128,128]{2,1,0:T(8,128)(2,1)} %param.10), kind=kOutput, calls=%fused_computation.22 | convolution fusion | flops 805306368 | bytes 25165824 | tf_op jit(solution)/shard_map/eij,ejm->eim/dot_general | solution.py:45
  176.8 12.6 %copy.43 = f32[192,128,128]{2,1,0:T(8,128)} copy(f32[192,128,128]{1,2,0:T(8,128)} %convolution_bitcast_fusion.2) | data formatting | bytes 25165824 | tf_op jit(solution)/shard_map/eij,ejm->eim/dot_general | solution.py:45
  189.3 16.4 %fusion.14 = f32[2,128,128]{2,1,0:T(8,128)S(1)} fusion(f32[6,128]{1,0:T(8,128)S(1)} %copy-done.3, s32[2,6]{1,0:T(2,128)S(1)} %multiply_add_fusion, s32[192]{0:T(256)S(1)} %get-tuple-element.12, f32[24,8,128,128]{3,2,1,0:T(8,128)} %bitcast.203), kind=kOutput, calls=%fused_computation.30 | convolution fusion | flops 453347584 | bytes 12717872 | tf_op jit(solution)/shard_map/dot_general | solution.py:48
  207.0 50.4 %reduce-scatter.7.cloned.1.call-done = f32[256,8]{0,1:T(8,128)} async-done(((f32[256,128]{0,1:T(8,128)}), f32[256,8]{0,1:T(8,128)}) %reduce-scatter.7.cloned.1.call-update) | async-done | bytes 8208 | tf_op jit(solution)/shard_map/reduce_scatter | solution.py:59
  258.4 22.2 %all_gather.23 = f32[256,128]{0,1:T(8,128)S(1)} all-gather(f32[256,8]{0,1:T(8,128)S(1)} %convolution_bitcast_fusion.6), channel_id=1, replica_groups=mesh['lag'=16,'pts'=2] {'lag'}, dimensions={1}, use_global_device_ids=true | all-gather | bytes 139264 | tf_op jit(solution)/shard_map/all_gather | solution.py:63
  285.1 9.6 %gather_fusion.2 = bf16[192,128,128]{2,1,0:T(8,128)(2,1)} fusion(bf16[6,4,128,128]{3,2,1,0:T(8,128)(2,1)S(1)} %pad_maximum_fusion.1, s32[192]{0:T(256)S(1)} %get-tuple-element.13), kind=kCustom, calls=%fused_computation.2 | custom fusion | bytes 12584448 | tf_op jit(solution)/shard_map/gather | solution.py:44
  294.7 13.7 %convolution_bitcast_fusion.1 = f32[192,128,128]{1,2,0:T(8,128)} fusion(bf16[192,128,128]{2,1,0:T(8,128)(2,1)} %gather_fusion.2, bf16[192,128,128]{2,1,0:T(8,128)(2,1)} %param.10), kind=kOutput, calls=%fused_computation.21 | convolution fusion | flops 805306368 | bytes 25165824 | tf_op jit(solution)/shard_map/eij,ejm->eim/dot_general | solution.py:45
  308.4 12.6 %copy.51 = f32[192,128,128]{2,1,0:T(8,128)} copy(f32[192,128,128]{1,2,0:T(8,128)} %convolution_bitcast_fusion.1) | data formatting | bytes 25165824 | tf_op jit(solution)/shard_map/eij,ejm->eim/dot_general | solution.py:45
  321.0 16.2 %fusion.13 = f32[2,128,128]{2,1,0:T(8,128)S(1)} fusion(f32[6,128]{1,0:T(8,128)S(1)} %copy-done.3, s32[2,6]{1,0:T(2,128)S(1)} %multiply_add_fusion, s32[192]{0:T(256)S(1)} %get-tuple-element.12, f32[24,8,128,128]{3,2,1,0:T(8,128)} %bitcast.204), kind=kOutput, calls=%fused_computation.29 | convolution fusion | flops 453347584 | bytes 12717872 | tf_op jit(solution)/shard_map/dot_general | solution.py:48
  338.3 50.5 %reduce-scatter.9.cloned.1.call-done = f32[256,8]{0,1:T(8,128)} async-done(((f32[256,128]{0,1:T(8,128)}), f32[256,8]{0,1:T(8,128)}) %reduce-scatter.9.cloned.1.call-update) | async-done | bytes 8208 | tf_op jit(solution)/shard_map/reduce_scatter | solution.py:59
  389.8 22.2 %all_gather.25 = f32[256,128]{0,1:T(8,128)S(1)} all-gather(f32[256,8]{0,1:T(8,128)S(1)} %convolution_bitcast_fusion.5), channel_id=1, replica_groups=mesh['lag'=16,'pts'=2] {'lag'}, dimensions={1}, use_global_device_ids=true | all-gather | bytes 139264 | tf_op jit(solution)/shard_map/all_gather | solution.py:63
  416.4 9.7 %gather_fusion.3 = bf16[192,128,128]{2,1,0:T(8,128)(2,1)} fusion(bf16[6,4,128,128]{3,2,1,0:T(8,128)(2,1)S(1)} %pad_maximum_fusion.2, s32[192]{0:T(256)S(1)} %get-tuple-element.13), kind=kCustom, calls=%fused_computation.3 | custom fusion | bytes 12584448 | tf_op jit(solution)/shard_map/gather | solution.py:44
  426.1 13.7 %convolution_bitcast_fusion = f32[192,128,128]{1,2,0:T(8,128)} fusion(bf16[192,128,128]{2,1,0:T(8,128)(2,1)} %gather_fusion.3, bf16[192,128,128]{2,1,0:T(8,128)(2,1)} %param.10), kind=kOutput, calls=%fused_computation.20 | convolution fusion | flops 805306368 | bytes 25165824 | tf_op jit(solution)/shard_map/eij,ejm->eim/dot_general | solution.py:45
  439.8 12.6 %copy.59 = f32[192,128,128]{2,1,0:T(8,128)} copy(f32[192,128,128]{1,2,0:T(8,128)} %convolution_bitcast_fusion) | data formatting | bytes 25165824 | tf_op jit(solution)/shard_map/eij,ejm->eim/dot_general | solution.py:45
  452.4 16.2 %fusion.12 = f32[2,128,128]{2,1,0:T(8,128)S(1)} fusion(f32[6,128]{1,0:T(8,128)S(1)} %copy-done.3, s32[2,6]{1,0:T(2,128)S(1)} %multiply_add_fusion, s32[192]{0:T(256)S(1)} %get-tuple-element.12, f32[24,8,128,128]{3,2,1,0:T(8,128)} %bitcast.201), kind=kOutput, calls=%fused_computation.28 | convolution fusion | flops 453347584 | bytes 12717872 | tf_op jit(solution)/shard_map/dot_general | solution.py:48
  469.6 50.7 %reduce-scatter.11.cloned.1.call-done = f32[256,8]{0,1:T(8,128)} async-done(((f32[256,128]{0,1:T(8,128)}), f32[256,8]{0,1:T(8,128)}) %reduce-scatter.11.cloned.1.call-update) | async-done | bytes 8208 | tf_op jit(solution)/shard_map/reduce_scatter | solution.py:59
  521.3 22.2 %all_gather.27 = f32[256,128]{0,1:T(8,128)S(1)} all-gather(f32[256,8]{0,1:T(8,128)S(1)} %convolution_bitcast_fusion.4), channel_id=1, replica_groups=mesh['lag'=16,'pts'=2] {'lag'}, dimensions={1}, use_global_device_ids=true | all-gather | bytes 139264 | tf_op jit(solution)/shard_map/all_gather | solution.py:63
  (67 shorter events, 34.7 us)
Async XLA Ops:
  6.5 119.1 %copy-start = (f32[256,128]{1,0:T(8,128)S(1)}, f32[256,128]{1,0:T(8,128)}, u32[]{:S(2)}) copy-start(f32[256,128]{1,0:T(8,128)} %param.15) | copy-start | bytes 393220
  6.5 119.1 %reduce-scatter.5.cloned.1.call-start = ((), (), s32[]{:S(2)}) async-start(), calls=%async_computation.4 | async-start | bytes 139264 | tf_op jit(solution)/shard_map/reduce_scatter | solution.py:59
  7.8 145.4 %collective-permute-start = (bf16[512,128]{0,1:T(8,128)(2,1)S(1)}, bf16[512,128]{0,1:T(8,128)(2,1)S(1)}, u32[]{:S(2)}, u32[]{:S(2)}) collective-permute-start(bf16[512,128]{0,1:T(8,128)(2,1)S(1)} %bitcast.223), channel_id=1, source_target_pairs={{0,2},{2,4},{4,6},{6,8},{8,10},{10,12},{12,14},{14,16},{16,18},{18... | collective-permute-start | bytes 393224 | tf_op jit(solution)/shard_map/ppermute | solution.py:12
  12.4 272.4 %collective-permute-start.1 = (bf16[512,128]{0,1:T(8,128)(2,1)S(1)}, bf16[512,128]{0,1:T(8,128)(2,1)S(1)}, u32[]{:S(2)}, u32[]{:S(2)}) collective-permute-start(bf16[512,128]{0,1:T(8,128)(2,1)S(1)} %bitcast.222), channel_id=1, source_target_pairs={{0,2},{2,4},{4,6},{6,8},{8,10},{10,12},{12,14},{14,16},{16,18},{18... | collective-permute-start | bytes 393224 | tf_op jit(solution)/shard_map/ppermute | solution.py:12
  14.4 401.8 %collective-permute-start.2 = (bf16[512,128]{0,1:T(8,128)(2,1)S(1)}, bf16[512,128]{0,1:T(8,128)(2,1)S(1)}, u32[]{:S(2)}, u32[]{:S(2)}) collective-permute-start(bf16[512,128]{0,1:T(8,128)(2,1)S(1)} %bitcast.221), channel_id=1, source_target_pairs={{0,2},{2,4},{4,6},{6,8},{8,10},{10,12},{12,14},{14,16},{16,18},{18... | collective-permute-start | bytes 393224 | tf_op jit(solution)/shard_map/ppermute | solution.py:12
  43.0 12.6 %copy-start.3 = (f32[6,128]{1,0:T(8,128)S(1)}, f32[6,128]{1,0:T(8,128)}, u32[]{:S(2)}) copy-start(f32[6,128]{1,0:T(8,128)} %param.14) | copy-start | bytes 9220
  55.6 17.1 %copy-start.2 = (bf16[4,256,128]{2,1,0:T(8,128)(2,1)S(1)}, bf16[4,256,128]{2,1,0:T(8,128)(2,1)}, u32[]{:S(2)}) copy-start(bf16[4,256,128]{2,1,0:T(8,128)(2,1)} %param.9) | copy-start | bytes 786436
  55.6 17.1 %copy-start.1 = (bf16[6,512,128]{2,1,0:T(8,128)(2,1)S(1)}, bf16[6,512,128]{2,1,0:T(8,128)(2,1)}, u32[]{:S(2)}) copy-start(bf16[6,512,128]{2,1,0:T(8,128)(2,1)} %param.8) | copy-start | bytes 2359300
  72.7 184.7 %reduce-scatter.7.cloned.1.call-start = ((), (), s32[]{:S(2)}) async-start(), calls=%async_computation.5 | async-start | bytes 139264 | tf_op jit(solution)/shard_map/reduce_scatter | solution.py:59
  206.6 182.2 %reduce-scatter.9.cloned.1.call-start = ((), (), s32[]{:S(2)}) async-start(), calls=%async_computation.6 | async-start | bytes 139264 | tf_op jit(solution)/shard_map/reduce_scatter | solution.py:59
  337.9 182.4 %reduce-scatter.11.cloned.1.call-start = ((), (), s32[]{:S(2)}) async-start(), calls=%async_computation.7 | async-start | bytes 139264 | tf_op jit(solution)/shard_map/reduce_scatter | solution.py:59
Sparse Core Ops, SparseCore 0:
  72.8 52.8 reduce-scatter.4
  206.7 50.6 reduce-scatter.6
  338.0 50.7 reduce-scatter.8
  469.6 50.6 reduce-scatter.10
where the time goes:
time: 558 us; the launch traced here: 552 us
  waiting for transfers between devices  204 us (37%)
  matrix products  124 us (22%)
  blocking collectives  101 us (18%)
  local copies, waits for them, and re-layouts  96.3 us (17%)
  between operations  13.9 us (2%)
  starting transfers between devices  10.1 us (2%)
    reduce_scatter x4, waiting for transfers between devices, per_device(): lax.psum_scatter(partial_field, 'lag', scatter_dimension=1, tiled=True)  204 us
    all_gather x4, blocking collectives, per_device(): lax.all_gather(apply_inverse(inverse_blocks, net_share), 'lag', axis=1, t...  88.8 us
    dot_general x4, matrix products, per_device(): jnp.dot(selector, products.reshape(entries, block_size * mode_cols), prec...  65.1 us
    dot_general x4, matrix products, per_device(): jnp.einsum('eij,ejm->eim', kernel_blocks, picked, preferred_element_type=...  54.8 us
    dot_general x4, local copies, waits for them, and re-layouts, per_device(): jnp.einsum('eij,ejm->eim', kernel_blocks, picked, preferred_element_type=...  50.4 us
    gather x4, local copies, waits for them, and re-layouts, per_device(): picked = by_block[lag_offset, block_col]  39.5 us
    all_gather x3, blocking collectives, per_device(): gathered = lax.all_gather(new_slab, 'pts', axis=0, tiled=True)  12.6 us
  transfers between devices with their start and end apart: 7, of which 4 were waited for; matrix products, arithmetic and copies ran while one was open for 30% of the time, Pallas kernels for 0%

commit v1 on v0

v1 whole, which is shorter than its diff:
```python
import functools
import jax
import jax.numpy as jnp
from jax import lax
from jax.experimental import pallas as pl
from jax.experimental.pallas import tpu as pltpu
from jax.sharding import PartitionSpec as P

STEPS = 4
BACK = STEPS - 1
MESH = pl.DeviceIdType.MESH
HIGHEST = lax.Precision.HIGHEST
VMEM_BYTES = 48 * 1024 * 1024


def split_dot(pair, x):
    both = jnp.dot(pair, x, preferred_element_type=jnp.float32)
    half = both.shape[0] // 2
    return both[:half] + both[half:]


def split_rows(value):
    head = value.astype(jnp.bfloat16)
    rest = (value - head.astype(jnp.float32)).astype(jnp.bfloat16)
    return head, rest


def history_kernel(
    chunk, row_ref, col_ref, lag_ref, k_ref, hist_ref, mk_ref, part_ref, pair_ref, even, odd, work
):
    step = pl.program_id(0)
    lags, rows, points = even.shape
    size = k_ref.shape[1]
    modes = hist_ref.shape[2]

    @pl.when(step == 0)
    def _():
        even[...] = jnp.zeros_like(even)
        odd[...] = jnp.zeros_like(odd)

    def add(total, i):
        e = step * chunk + i
        r = pl.multiple_of(row_ref[e] * size, size)
        c = pl.multiple_of(col_ref[e] * size, size)
        total[lag_ref[e], pl.ds(r, size), pl.ds(c, size)] += k_ref[i].astype(jnp.float32)

    def body(j, carry):
        add(even, 2 * j)
        add(odd, 2 * j + 1)
        return carry

    lax.fori_loop(0, chunk // 2, body, 0, unroll=2)

    @pl.when(step == pl.num_programs(0) - 1)
    def _():
        for l in range(lags):
            head, rest = split_rows(even[l] + odd[l])
            target = pair_ref.at[l] if l < BACK else work
            target[:rows, :] = head
            target[rows:, :] = rest
            count = min(l, BACK) + 1
            x = jnp.concatenate([hist_ref[l - s] for s in range(count)], axis=1)
            found = split_dot(target[...], x)
            for s in range(STEPS):
                if s < count:
                    term = found[:, s * modes:(s + 1) * modes] * mk_ref[l:l + 1, :]
                    if l == s:
                        part_ref[s] = term
                    else:
                        part_ref[s] += term


def march_kernel(
    n, group, groups, n_pts,
    part_ref, pair_ref, halo_ref, mk_ref, inc_ref, inv_ref, out_ref,
    field, got1, sum1, got2, sum2, root_field, solved_pair, slabs, full,
    s1, r1, s2, r2, s3, r3, s4, r4, s5, r5, s6, r6, sx, rx,
):
    me = lax.axis_index("lag")
    mine = lax.axis_index("pts")
    g = lax.rem(me, group)
    z = me // group
    rows = part_ref.shape[1]
    modes = part_ref.shape[2]
    points = halo_ref.shape[1]
    size = inv_ref.shape[1]
    row_blocks = rows // size
    wide = rows // group
    thin = rows // n
    is_root = me == 0

    barrier = pltpu.get_barrier_semaphore()

    def greet(k, carry):
        pl.semaphore_signal(
            barrier, inc=1, device_id={"lag": lax.rem(me + k, n)}, device_id_type=MESH
        )
        return carry

    lax.fori_loop(1, n, greet, 0)

    for k in range(1, n_pts):
        pl.semaphore_signal(
            barrier, inc=1, device_id={"pts": lax.rem(mine + k, n_pts)}, device_id_type=MESH
        )

    def to(device, src, dst, send, recv):
        return pltpu.make_async_remote_copy(
            src_ref=src, dst_ref=dst, send_sem=send, recv_sem=recv,
            device_id=device, device_id_type=MESH,
        )

    def in_group(k):
        return lax.rem(g + k, group)

    def in_column(k):
        return lax.rem(z + k, groups)

    def span(first, count):
        return pl.ds(pl.multiple_of(first * count, count), count)

    other = {"lag": lax.rem(me + 1, n)}

    def copies1(s):
        for k in range(1, group):
            peer = in_group(k)
            yield to({"lag": z * group + peer}, field.at[s, span(peer, wide)],
                     got1.at[s, k - 1], s1.at[s, k - 1], r1.at[s])

    def copies2(s):
        for k in range(1, groups):
            peer = in_column(k)
            yield to({"lag": peer * group + g}, sum1.at[s, span(peer, thin)],
                     got2.at[s, k - 1], s2.at[s, k - 1], r2.at[s])

    share = span(g * groups + z, thin)

    def copy3(s):
        return to({"lag": 0}, sum2.at[s], root_field.at[s, share], s3.at[s], r3.at[s])

    def local_part(s):
        total = part_ref[s]
        for l in range(s):
            total += mk_ref[l:l + 1, :] * split_dot(pair_ref[l], halo_ref[BACK + l - s])
        field[s] = total

    def reduce1(s):
        for copy in copies1(s):
            copy.start()

    def reduce2(s):
        to(other, got1.at[s], got1.at[s], s1.at[s, 0], r1.at[s]).wait_recv()
        total = field[s, span(g, wide), :]
        for k in range(group - 1):
            total += got1[s, k]
        sum1[s] = total
        for copy in copies2(s):
            copy.start()

    def reduce3(s):
        to(other, got2.at[s], got2.at[s], s2.at[s, 0], r2.at[s]).wait_recv()
        total = sum1[s, span(z, thin), :]
        for k in range(groups - 1):
            total += got2[s, k]

        @pl.when(is_root)
        def _():
            root_field[s, 0:thin, :] = total

        @pl.when(jnp.logical_not(is_root))
        def _():
            sum2[s] = total
            copy3(s).start()

    def solve(value, r):
        return jnp.dot(inv_ref[r * size:(r + 1) * size, :], value,
                       precision=HIGHEST, preferred_element_type=jnp.float32)

    def solve_pairs():
        for l in range(BACK):
            for r in range(row_blocks):
                block = slice(r * size, (r + 1) * size)
                below = slice(rows + r * size, rows + (r + 1) * size)
                value = (pair_ref[l, block, :].astype(jnp.float32)
                         + pair_ref[l, below, :].astype(jnp.float32))
                head, rest = split_rows(solve(value, r))
                solved_pair[l, block, :] = head
                solved_pair[l, below, :] = rest

    def copies_x(s):
        for k in range(1, n_pts):
            here = slabs.at[s, span(mine, rows)]
            yield to({"pts": lax.rem(mine + k, n_pts)}, here, here, sx.at[s, k - 1], rx.at[s])

    def copy4(s, j):
        part = span(lax.rem(j, group) * groups + j // group, thin)
        return to({"lag": j}, full.at[s, part], full.at[s, part], s4.at[s], r4.at[s])

    def copies5(s):
        for k in range(1, groups):
            peer = in_column(k) * group + g
            here = full.at[s, share]
            yield peer, to({"lag": peer}, here, here, s5.at[s, k - 1], r5.at[s])

    def copies6(s):
        for k in range(1, group):
            peer = z * group + in_group(k)
            here = full.at[s, span(g, wide)]
            yield peer, to({"lag": peer}, here, here, s6.at[s, k - 1], r6.at[s])

    def march(s):
        rest = root_field.at[s, pl.ds(thin, rows - thin)]
        to(other, rest, rest, s3.at[s], r3.at[s]).wait_recv()
        net = inc_ref[s].astype(jnp.float32) - root_field[s]
        total = jnp.concatenate(
            [solve(net[r * size:(r + 1) * size], r) for r in range(row_blocks)], axis=0)
        for l in range(s - 1, -1, -1):
            if l == 0:
                away = slabs.at[s - 1, pl.ds(0, points - rows)]
                to(other, away, away, sx.at[s - 1, 0], rx.at[s - 1]).wait_recv()
            total -= mk_ref[l:l + 1, :] * split_dot(solved_pair[l], slabs[s - 1 - l])
        if s < BACK:
            slabs[s, span(mine, rows), :] = total.astype(jnp.bfloat16)
            for copy in copies_x(s):
                copy.start()
        full[s] = total

        def hand(j, carry):
            copy4(s, j).start()
            return carry

        lax.fori_loop(1, n, hand, 0)
        for unused, copy in copies5(s):
            copy.start()
        for unused, copy in copies6(s):
            copy.start()

    def spread(s):
        to(other, full.at[s, share], full.at[s, share], s4.at[s], r4.at[s]).wait_recv()
        for peer, copy in copies5(s):
            @pl.when(peer != 0)
            def _(copy=copy):
                copy.start()
        away = full.at[s, pl.ds(0, (groups - 1) * thin)]
        to(other, away, away, s5.at[s, 0], r5.at[s]).wait_recv()
        for peer, copy in copies6(s):
            @pl.when(peer != 0)
            def _(copy=copy):
                copy.start()

    local_part(0)
    pl.semaphore_wait(barrier, n + n_pts - 2)
    reduce1(0)
    for s in range(1, STEPS):
        local_part(s)
        reduce1(s)

    @pl.when(is_root)
    def _():
        solve_pairs()

    reduce2(0)
    reduce2(1)
    reduce3(0)
    for s in range(STEPS):
        @pl.when(is_root)
        def _(s=s):
            march(s)

        if s + 2 < STEPS:
            reduce2(s + 2)
        if s + 1 < STEPS:
            reduce3(s + 1)

    @pl.when(jnp.logical_not(is_root))
    def _():
        for s in range(STEPS):
            spread(s)
        for s in range(STEPS):
            away = full.at[s, pl.ds(0, (group - 1) * wide)]
            to(other, away, away, s6.at[s, 0], r6.at[s]).wait_recv()

    out_ref[...] = full[...]

    for s in range(STEPS):
        for copy in copies1(s):
            copy.wait_send()
        for copy in copies2(s):
            copy.wait_send()

        @pl.when(is_root)
        def _(s=s):
            if s < BACK:
                for copy in copies_x(s):
                    copy.wait_send()
            rest = full.at[s, pl.ds(thin, rows - thin)]
            to(other, rest, rest, s4.at[s], r4.at[s]).wait_send()

        @pl.when(jnp.logical_not(is_root))
        def _(s=s):
            copy3(s).wait_send()

        for peer, copy in [*copies5(s), *copies6(s)]:
            @pl.when(jnp.logical_or(is_root, peer != 0))
            def _(copy=copy):
                copy.wait_send()


def per_device(
    n, n_pts, history, incident, kernel_blocks, block_row, block_col, lag_offset, mode_kernel,
    self_inverse,
):
    lags, points, modes = history.shape
    entries, size = kernel_blocks.shape[0], kernel_blocks.shape[1]
    rows = self_inverse.shape[0]
    f32, bf16 = jnp.float32, jnp.bfloat16
    vmem = pl.BlockSpec(memory_space=pltpu.VMEM)
    smem = pl.BlockSpec(memory_space=pltpu.SMEM)
    chunks = 8
    chunk = entries // chunks

    halo = lax.ppermute(history[lags - BACK:], "lag", [(i, i + 1) for i in range(n - 1)])

    part, pair = pl.pallas_call(
        functools.partial(history_kernel, chunk),
        grid=(chunks,),
        out_shape=(
            jax.ShapeDtypeStruct((STEPS, rows, modes), f32),
            jax.ShapeDtypeStruct((BACK, 2 * rows, points), bf16),
        ),
        in_specs=[
            smem, smem, smem,
            pl.BlockSpec((chunk, size, size), lambda i: (i, 0, 0)),
            vmem, vmem,
        ],
        out_specs=(vmem, vmem),
        scratch_shapes=[
            pltpu.VMEM((lags, rows, points), f32),
            pltpu.VMEM((lags, rows, points), f32),
            pltpu.VMEM((2 * rows, points), bf16),
        ],
        compiler_params=pltpu.CompilerParams(vmem_limit_bytes=VMEM_BYTES),
        cost_estimate=pl.CostEstimate(
            flops=4 * lags * rows * points * STEPS * modes,
            bytes_accessed=entries * size * size * 2 + lags * points * modes * 2,
            transcendentals=0),
    )(block_row, block_col, lag_offset, kernel_blocks, history, mode_kernel)

    group = 4 if n % 4 == 0 else 1
    groups = n // group
    wide, thin = rows // group, rows // n
    dma = pltpu.SemaphoreType.DMA
    peers, tops, sides = max(group - 1, 1), max(groups - 1, 1), max(n_pts - 1, 1)
    return pl.pallas_call(
        functools.partial(march_kernel, n, group, groups, n_pts),
        out_shape=jax.ShapeDtypeStruct((STEPS, rows, modes), f32),
        in_specs=[vmem] * 6,
        out_specs=vmem,
        scratch_shapes=[
            pltpu.VMEM((STEPS, rows, modes), f32),
            pltpu.VMEM((STEPS, peers, wide, modes), f32),
            pltpu.VMEM((STEPS, wide, modes), f32),
            pltpu.VMEM((STEPS, tops, thin, modes), f32),
            pltpu.VMEM((STEPS, thin, modes), f32),
            pltpu.VMEM((STEPS, rows, modes), f32),
            pltpu.VMEM((BACK, 2 * rows, points), bf16),
            pltpu.VMEM((BACK, points, modes), bf16),
            pltpu.VMEM((STEPS, rows, modes), f32),
            dma((STEPS, peers)), dma((STEPS,)),
            dma((STEPS, tops)), dma((STEPS,)),
            dma((STEPS,)), dma((STEPS,)),
            dma((STEPS,)), dma((STEPS,)),
            dma((STEPS, tops)), dma((STEPS,)),
            dma((STEPS, peers)), dma((STEPS,)),
            dma((BACK, sides)), dma((BACK,)),
        ],
        compiler_params=pltpu.CompilerParams(
            collective_id=0, has_side_effects=True, vmem_limit_bytes=VMEM_BYTES),
    )(part, pair, halo, mode_kernel, incident, self_inverse)


def solution(mesh):
    return jax.shard_map(
        functools.partial(per_device, mesh.shape["lag"], mesh.shape["pts"]),
        mesh=mesh,
        in_specs=(
            P("lag", None, None),
            P(None, "pts", None),
            P(("lag", "pts"), None, None),
            P(("lag", "pts")),
            P(("lag", "pts")),
            P(("lag", "pts")),
            P("lag", None),
            P("pts", None),
        ),
        out_specs=P(None, "pts", None),
        check_vma=False,
    )
```

time: 558 us -> 59.8 us (0.11); the launches traced: 552 us -> 59.4 us
  waiting for transfers between devices: 204 us -> 0.01 us
  matrix products: 124 us -> 0 us
  blocking collectives: 101 us -> 0 us
  local copies, waits for them, and re-layouts: 96.3 us -> 5.73 us
  Pallas kernels: 0 us -> 49.1 us
  between operations: 13.9 us -> 0.07 us
  starting transfers between devices: 10.1 us -> 4.51 us
    reduce_scatter x4 -> x0, waiting for transfers between devices: 204 us -> none  [per_device(): lax.psum_scatter(partial_field, 'lag', scatter_dimension=1, tiled=True)]
    dot_general x12 -> x0, matrix products: 124 us -> none  [the longest x4 65.1 us: per_device(): jnp.dot(selector, products.reshape(entries, block_size * mode_cols), prec...]
    all_gather x7 -> x0, blocking collectives: 101 us -> none  [the longest x4 88.8 us: per_device(): lax.all_gather(apply_inverse(inverse_blocks, net_share), 'lag', axis=1, t...]
    dot_general x4 -> x0, local copies, waits for them, and re-layouts: 50.4 us -> none  [per_device(): jnp.einsum('eij,ejm->eim', kernel_blocks, picked, preferred_element_type=...]
    pallas_call x0 -> x2, Pallas kernels: none -> 49.1 us  [the longest x1 40.8 us: per_device(): pl.pallas_call(functools.partial(march_kernel, n, group, groups, n_pts),...]
    gather x4 -> x0, local copies, waits for them, and re-layouts: 39.5 us -> none  [per_device(): picked = by_block[lag_offset, block_col]]
  transfers between devices with their start and end apart: 7 -> 1, of which waited for: 4 -> 0; matrix products, arithmetic and copies ran while one was open for 30% -> 0% of each run, Pallas kernels for 0% -> 14%
where the time goes in v1:
time: 59.8 us; the launch traced here: 59.4 us
  Pallas kernels  49.1 us (82%)
  local copies, waits for them, and re-layouts  5.73 us (10%)
  starting transfers between devices  4.51 us (8%)
    pallas_call x1, Pallas kernels, per_device(): pl.pallas_call(functools.partial(march_kernel, n, group, groups, n_pts),...  40.8 us
    pallas_call x1, Pallas kernels, per_device(): pl.pallas_call(functools.partial(history_kernel, chunk), grid=(chunks,),...  8.29 us
    unnamed x15, local copies, waits for them, and re-layouts  4.65 us
    ppermute x1, starting transfers between devices, per_device(): lax.ppermute(history[lags - BACK:], 'lag', [(i, i + 1) for i in range(n -...  4.51 us
  transfers between devices with their start and end apart: 1, of which 0 were waited for; matrix products, arithmetic and copies ran while one was open for 0% of the time, Pallas kernels for 14%

profile of v1, /device:TPU:1, one launch (start us, length us, event | category | flops | bytes accessed | tf_op | source)
XLA Modules:
  0.0 59.4 jit_solution(5738244148889429911)
XLA Ops:
  0.0 0.0 copy-start.2
  0.0 0.0 copy-start.1
  0.0 1.1 %slice.3 = bf16[3,512,128]{2,1,0:T(8,128)(2,1)S(1)} slice(bf16[6,512,128]{2,1,0:T(8,128)(2,1)} %hist_ref.1), slice={[3:6], [0:512], [0:128]} | slice | bytes 786432 | tf_op jit(solution)/shard_map/slice | solution.py:322
  1.1 4.5 %collective-permute-start = (bf16[3,512,128]{2,1,0:T(8,128)(2,1)S(1)}, bf16[3,512,128]{2,1,0:T(8,128)(2,1)S(1)}, u32[]{:S(2)}, u32[]{:S(2)}) collective-permute-start(bf16[3,512,128]{2,1,0:T(8,128)(2,1)S(1)} %slice.3), channel_id=1, source_target_pairs={{0,2},{2,4},{4,6},{6,8},{8,10},{10,12},{12,14},{14,16},{16,18},{18... | collective-permute-start | bytes 1179656 | tf_op jit(solution)/shard_map/ppermute | solution.py:322
  5.6 0.0 copy-start
  5.6 1.1 %copy-done = bf16[6,512,128]{2,1,0:T(8,128)(2,1)S(1)} copy-done((bf16[6,512,128]{2,1,0:T(8,128)(2,1)S(1)}, bf16[6,512,128]{2,1,0:T(8,128)(2,1)}, u32[]{:S(2)}) %copy-start) | copy-done | bytes 786456
  6.7 0.0 copy-start.3
  6.7 0.7 %copy-done.3 = f32[6,128]{1,0:T(8,128)S(1)} copy-done((f32[6,128]{1,0:T(8,128)S(1)}, f32[6,128]{1,0:T(8,128)}, u32[]{:S(2)}) %copy-start.3) | copy-done | bytes 3096
  7.4 0.0 copy-start.4
  7.4 0.7 %copy-done.4 = s32[192]{0:T(256)S(1)} copy-done((s32[192]{0:T(256)S(1)}, s32[192]{0:T(256)}, u32[]{:S(2)}) %copy-start.4) | copy-done | bytes 792
  8.1 0.0 copy-start.5
  8.1 0.7 %copy-done.5 = s32[192]{0:T(256)S(1)} copy-done((s32[192]{0:T(256)S(1)}, s32[192]{0:T(256)}, u32[]{:S(2)}) %copy-start.5) | copy-done | bytes 792
  8.8 0.0 copy-start.6
  8.8 0.7 %copy-done.6 = s32[192]{0:T(256)S(1)} copy-done((s32[192]{0:T(256)S(1)}, s32[192]{0:T(256)}, u32[]{:S(2)}) %copy-start.6) | copy-done | bytes 792
  9.5 8.3 %shard_map.82 = (f32[4,256,128]{2,1,0:T(8,128)S(1)}, bf16[3,512,512]{2,1,0:T(8,128)(2,1)S(1)}) custom-call(s32[192]{0:T(256)S(1)} %copy-done.4, s32[192]{0:T(256)S(1)} %copy-done.5, s32[192]{0:T(256)S(1)} %copy-done.6, bf16[192,128,128]{2,1,0:T(8,128)(2,1)} %k_ref.1, bf16[6,512,128]{2,1,0:T(8,128)(2,1)S(1)} %copy-done, f32[6,128]{1,0:T(8,128)S(1)} %copy-done.3), custom_call_target="tpu_custom_call" | custom-call | flops 1610612736 | bytes 7077888 | tf_op jit(solution)/shard_map/pallas_call | solution.py:324
  17.8 0.0 collective-permute-done.halo_ref
  17.8 0.0 copy-done.2
  17.8 0.0 copy-done.1
  17.8 40.8 %shard_map.83 = f32[4,256,128]{2,1,0:T(8,128)S(1)} custom-call(f32[4,256,128]{2,1,0:T(8,128)S(1)} %get-tuple-element.7.part_ref, bf16[3,512,512]{2,1,0:T(8,128)(2,1)S(1)} %get-tuple-element.8.pair_ref, bf16[3,512,128]{2,1,0:T(8,128)(2,1)S(1)} %collective-permute-done.halo_ref, f32[6,128]{1,0:T(8,128)S(1)} %copy-done.3, bf16[4,256,128]{2,1,0:T(8,128)(2,1)S(1)} %copy-done.1, ...), custom_call_target="tpu_custom_call" | custom-call | tf_op jit(solution)/shard_map/pallas_call | solution.py:354
  58.6 0.8 %copy.10 = f32[4,256,128]{2,1,0:T(8,128)} copy(f32[4,256,128]{2,1,0:T(8,128)S(1)} %shard_map.83) | data formatting | bytes 1048576
Async XLA Ops:
  0.0 17.8 %copy-start.2 = (f32[256,128]{1,0:T(8,128)S(1)}, f32[256,128]{1,0:T(8,128)}, u32[]{:S(2)}) copy-start(f32[256,128]{1,0:T(8,128)} %inv_ref.1) | copy-start | bytes 393220
  0.0 17.8 %copy-start.1 = (bf16[4,256,128]{2,1,0:T(8,128)(2,1)S(1)}, bf16[4,256,128]{2,1,0:T(8,128)(2,1)}, u32[]{:S(2)}) copy-start(bf16[4,256,128]{2,1,0:T(8,128)(2,1)} %inc_ref.1) | copy-start | bytes 786436
  1.1 16.7 %collective-permute-start = (bf16[3,512,128]{2,1,0:T(8,128)(2,1)S(1)}, bf16[3,512,128]{2,1,0:T(8,128)(2,1)S(1)}, u32[]{:S(2)}, u32[]{:S(2)}) collective-permute-start(bf16[3,512,128]{2,1,0:T(8,128)(2,1)S(1)} %slice.3), channel_id=1, source_target_pairs={{0,2},{2,4},{4,6},{6,8},{8,10},{10,12},{12,14},{14,16},{16,18},{18... | collective-permute-start | bytes 1179656 | tf_op jit(solution)/shard_map/ppermute | solution.py:322
  5.6 1.1 %copy-start = (bf16[6,512,128]{2,1,0:T(8,128)(2,1)S(1)}, bf16[6,512,128]{2,1,0:T(8,128)(2,1)}, u32[]{:S(2)}) copy-start(bf16[6,512,128]{2,1,0:T(8,128)(2,1)} %hist_ref.1) | copy-start | bytes 2359300
  6.7 0.7 %copy-start.3 = (f32[6,128]{1,0:T(8,128)S(1)}, f32[6,128]{1,0:T(8,128)}, u32[]{:S(2)}) copy-start(f32[6,128]{1,0:T(8,128)} %mk_ref.3) | copy-start | bytes 9220
  7.4 0.7 %copy-start.4 = (s32[192]{0:T(256)S(1)}, s32[192]{0:T(256)}, u32[]{:S(2)}) copy-start(s32[192]{0:T(256)} %row_ref.1) | copy-start | bytes 2308
  8.1 0.7 %copy-start.5 = (s32[192]{0:T(256)S(1)}, s32[192]{0:T(256)}, u32[]{:S(2)}) copy-start(s32[192]{0:T(256)} %col_ref.1) | copy-start | bytes 2308
  8.8 0.7 %copy-start.6 = (s32[192]{0:T(256)S(1)}, s32[192]{0:T(256)}, u32[]{:S(2)}) copy-start(s32[192]{0:T(256)} %lag_ref.1) | copy-start | bytes 2308

commit v2 on v1

v2 whole, which is shorter than its diff:
```python
import functools
import jax
import jax.numpy as jnp
from jax import lax
from jax.experimental import pallas as pl
from jax.experimental.pallas import tpu as pltpu
from jax.sharding import PartitionSpec as P

STEPS = 4
BACK = STEPS - 1
MESH = pl.DeviceIdType.MESH
VMEM_BYTES = 56 * 1024 * 1024


def split_dot(pair, x):
    both = jnp.dot(pair, x, preferred_element_type=jnp.float32)
    half = both.shape[0] // 2
    return both[:half] + both[half:]


def split_rows(value):
    head = value.astype(jnp.bfloat16)
    rest = (value - head.astype(jnp.float32)).astype(jnp.bfloat16)
    return head, rest


def history_kernel(
    chunks, row_hbm, col_hbm, lag_hbm, k_hbm, hist_hbm, mk_hbm, part_ref, pair_ref,
    even, odd, work, row_ref, col_ref, lag_ref, k_ref, hist_ref, mk_ref, sem, k_sem,
):
    lags, rows, points = even.shape
    entries, size = k_ref.shape[0], k_ref.shape[1]
    modes = hist_ref.shape[2]
    chunk = entries // chunks
    pairs = [(row_hbm, row_ref), (col_hbm, col_ref), (lag_hbm, lag_ref),
             (hist_hbm, hist_ref), (mk_hbm, mk_ref)]
    loads = [pltpu.make_async_copy(src, dst, sem.at[i]) for i, (src, dst) in enumerate(pairs)]

    def load_k(c):
        span = pl.ds(c * chunk, chunk)
        return pltpu.make_async_copy(k_hbm.at[span], k_ref.at[span], k_sem.at[c])

    for copy in loads[:3]:
        copy.start()
    for c in range(chunks):
        load_k(c).start()
    for copy in loads[3:]:
        copy.start()
    even[...] = jnp.zeros_like(even)
    odd[...] = jnp.zeros_like(odd)
    for copy in loads[:3]:
        copy.wait()

    def add(total, e):
        r = pl.multiple_of(row_ref[e] * size, size)
        c = pl.multiple_of(col_ref[e] * size, size)
        total[lag_ref[e], pl.ds(r, size), pl.ds(c, size)] += k_ref[e].astype(jnp.float32)

    def take(c, carry):
        load_k(c).wait()

        def body(j, carry):
            add(even, c * chunk + 2 * j)
            add(odd, c * chunk + 2 * j + 1)
            return carry

        return lax.fori_loop(0, chunk // 2, body, carry, unroll=2)

    lax.fori_loop(0, chunks, take, 0)
    for copy in loads[3:]:
        copy.wait()
    for l in range(lags):
        head, rest = split_rows(even[l] + odd[l])
        target = pair_ref.at[l] if l < BACK else work
        target[:rows, :] = head
        target[rows:, :] = rest
        count = min(l, BACK) + 1
        x = jnp.concatenate([hist_ref[l - s] for s in range(count)], axis=1)
        found = split_dot(target[...], x)
        for s in range(count):
            term = found[:, s * modes:(s + 1) * modes] * mk_ref[l:l + 1, :]
            if l == s:
                part_ref[s] = term
            else:
                part_ref[s] += term


def march_kernel(
    n, group, groups, n_pts,
    part_ref, pair_ref, hist_hbm, mk_ref, inc_ref, inv_ref, out_ref,
    halo_ref, inv_pair, field, got1, sum1, got2, sum2, root_field, solved_pair, slabs, full,
    s1, r1, s2, r2, s3, r3, s4, r4, s5, r5, s6, r6, s7, r7, s8, sx, rx, sh, rh,
):
    me = lax.axis_index("lag")
    mine = lax.axis_index("pts")
    g = lax.rem(me, group)
    z = me // group
    rows = part_ref.shape[1]
    modes = part_ref.shape[2]
    points = halo_ref.shape[1]
    size = inv_ref.shape[1]
    row_blocks = rows // size
    wide = rows // group
    thin = rows // n
    is_root = me == 0
    lags = hist_hbm.shape[0]
    hubs = [1 if s < BACK and group > 1 else 0 for s in range(STEPS)]

    barrier = pltpu.get_barrier_semaphore()

    def greet(k, carry):
        pl.semaphore_signal(
            barrier, inc=1, device_id={"lag": lax.rem(me + k, n)}, device_id_type=MESH
        )
        return carry

    lax.fori_loop(1, n, greet, 0)

    for k in range(1, n_pts):
        pl.semaphore_signal(
            barrier, inc=1, device_id={"pts": lax.rem(mine + k, n_pts)}, device_id_type=MESH
        )

    def to(device, src, dst, send, recv):
        return pltpu.make_async_remote_copy(
            src_ref=src, dst_ref=dst, send_sem=send, recv_sem=recv,
            device_id=device, device_id_type=MESH,
        )

    def in_group(k):
        return lax.rem(g + k, group)

    def in_column(k):
        return lax.rem(z + k, groups)

    def span(first, count):
        return pl.ds(pl.multiple_of(first * count, count), count)

    other = {"lag": lax.rem(me + 1, n)}

    def copies1(s):
        for k in range(1, group):
            peer = in_group(k)
            yield to({"lag": z * group + peer}, field.at[s, span(peer, wide)],
                     got1.at[s, k - 1], s1.at[s, k - 1], r1.at[s])

    def copies2(s):
        for k in range(1, groups):
            peer = in_column(k)
            yield to({"lag": peer * group + g}, sum1.at[s, span(peer, thin)],
                     got2.at[s, k - 1], s2.at[s, k - 1], r2.at[s])

    share = span(g * groups + z, thin)

    def copy3(s):
        return to({"lag": 0}, sum2.at[s], root_field.at[s, share], s3.at[s], r3.at[s])

    def halo_copy(i):
        return to({"lag": lax.rem(me + 1, n)}, hist_hbm.at[lags - BACK + i], halo_ref.at[i],
                  sh.at[i], rh.at[i])

    def local_part(s):
        halo_copy(BACK - s).wait_recv()
        total = part_ref[s]
        for l in range(s):
            total += mk_ref[l:l + 1, :] * split_dot(pair_ref[l], halo_ref[BACK + l - s])
        field[s] = total

    def reduce1(s):
        for copy in copies1(s):
            copy.start()

    def reduce2(s):
        to(other, got1.at[s], got1.at[s], s1.at[s, 0], r1.at[s]).wait_recv()
        total = field[s, span(g, wide), :]
        for k in range(group - 1):
            total += got1[s, k]
        sum1[s] = total
        for copy in copies2(s):
            copy.start()

    def reduce3(s):
        to(other, got2.at[s], got2.at[s], s2.at[s, 0], r2.at[s]).wait_recv()
        total = sum1[s, span(z, thin), :]
        for k in range(groups - 1):
            total += got2[s, k]

        @pl.when(is_root)
        def _():
            root_field[s, 0:thin, :] = total

        @pl.when(jnp.logical_not(is_root))
        def _():
            sum2[s] = total
            copy3(s).start()

    def solve(head, rest, r):
        both = jnp.dot(inv_pair[r], head, preferred_element_type=jnp.float32)
        last = jnp.dot(inv_pair[r, :size, :], rest, preferred_element_type=jnp.float32)
        return both[:size] + both[size:] + last

    def solve_pair(l):
        for r in range(row_blocks):
            block = slice(r * size, (r + 1) * size)
            below = slice(rows + r * size, rows + (r + 1) * size)
            head, rest = split_rows(solve(pair_ref[l, block, :], pair_ref[l, below, :], r))
            solved_pair[l, block, :] = head
            solved_pair[l, below, :] = rest

    def copies_x(s):
        for k in range(1, n_pts):
            here = slabs.at[s, span(mine, rows)]
            yield to({"pts": lax.rem(mine + k, n_pts)}, here, here, sx.at[s, k - 1], rx.at[s])

    def copy4(s, j):
        part = span(lax.rem(j, group) * groups + j // group, thin)
        return to({"lag": j}, full.at[s, part], full.at[s, part], s4.at[s], r4.at[s])

    def copies5(s):
        for k in range(1, groups):
            peer = in_column(k) * group + g
            here = full.at[s, share]
            yield peer, to({"lag": peer}, here, here, s5.at[s, k - 1], r5.at[s])

    def copies6(s):
        for k in range(1, group):
            peer = z * group + in_group(k)
            here = full.at[s, span(g, wide)]
            yield peer, to({"lag": peer}, here, here, s6.at[s, k - 1], r6.at[s])

    def copies_for_root(s):
        here = full.at[s, pl.ds(0, thin)]
        for k in range(1, groups):
            yield to({"lag": k * group}, here, here, s8.at[s, k - 1], r5.at[s])
        here = full.at[s, pl.ds(0, wide)]
        for k in range(2, group):
            yield to({"lag": k}, here, here, s8.at[s, groups + k - 3], r6.at[s])

    def copy7(s):
        return to({"lag": hubs[s]}, full.at[s], full.at[s], s7.at[s], r7.at[s])

    def needs(s, peer):
        if hubs[s] == 0:
            return peer != 0
        return jnp.logical_and(peer != 0, peer != hubs[s])

    def hand_out(s):
        hub = hubs[s]

        def hand(j, carry):
            copy4(s, j).start()
            return carry

        lax.fori_loop(hub + 1, n, hand, 0)
        for peer, copy in [*copies5(s), *copies6(s)]:
            if hub == 0:
                copy.start()
            else:
                @pl.when(peer != 0)
                def _(copy=copy):
                    copy.start()
        if hub != 0:
            for copy in copies_for_root(s):
                copy.start()

    def march(s):
        if s > 0:
            rest = root_field.at[s, pl.ds(thin, rows - thin)]
            to(other, rest, rest, s3.at[s], r3.at[s]).wait_recv()
        net = inc_ref[s].astype(jnp.float32) - root_field[s]
        blocks = [split_rows(net[r * size:(r + 1) * size]) for r in range(row_blocks)]
        total = jnp.concatenate(
            [solve(head, rest, r) for r, (head, rest) in enumerate(blocks)], axis=0)
        for l in range(s - 1, -1, -1):
            if l == 0:
                away = slabs.at[s - 1, pl.ds(0, points - rows)]
                to(other, away, away, sx.at[s - 1, 0], rx.at[s - 1]).wait_recv()
            total -= mk_ref[l:l + 1, :] * split_dot(solved_pair[l], slabs[s - 1 - l])
        if s < BACK:
            slabs[s, span(mine, rows), :] = total.astype(jnp.bfloat16)
            for copy in copies_x(s):
                copy.start()
        full[s] = total
        if hubs[s] == 0:
            hand_out(s)
        else:
            copy7(s).start()

    def pass_on(s):
        def plain():
            to(other, full.at[s, share], full.at[s, share], s4.at[s], r4.at[s]).wait_recv()
            for peer, copy in copies5(s):
                @pl.when(needs(s, peer))
                def _(copy=copy):
                    copy.start()

        if hubs[s] == 0:
            plain()
        else:
            @pl.when(me == hubs[s])
            def _():
                copy7(s).wait_recv()
                hand_out(s)

            pl.when(me != hubs[s])(plain)

    def fill(s):
        def plain():
            away = full.at[s, pl.ds(0, (groups - 1) * thin)]
            to(other, away, away, s5.at[s, 0], r5.at[s]).wait_recv()
            for peer, copy in copies6(s):
                @pl.when(needs(s, peer))
                def _(copy=copy):
                    copy.start()

        if hubs[s] == 0:
            plain()
        else:
            pl.when(me != hubs[s])(plain)

    def finish(s):
        def plain():
            away = full.at[s, pl.ds(0, (group - 1) * wide)]
            to(other, away, away, s6.at[s, 0], r6.at[s]).wait_recv()

        if hubs[s] == 0:
            plain()
        else:
            pl.when(me != hubs[s])(plain)

    field[0] = part_ref[0]

    @pl.when(is_root)
    def _():
        for s in range(1, STEPS):
            field[s] = part_ref[s]
        for r in range(row_blocks):
            head, rest = split_rows(inv_ref[r * size:(r + 1) * size, :])
            inv_pair[r, :size, :] = head
            inv_pair[r, size:, :] = rest

    pl.semaphore_wait(barrier, n + n_pts - 2)
    reduce1(0)

    @pl.when(me < n - 1)
    def _():
        for i in range(BACK - 1, -1, -1):
            halo_copy(i).start()

    @pl.when(is_root)
    def _():
        for s in range(1, STEPS):
            reduce1(s)
        for l in range(BACK):
            solve_pair(l)
        reduce2(0)
        reduce3(0)
        rest = root_field.at[0, pl.ds(thin, rows - thin)]
        to(other, rest, rest, s3.at[0], r3.at[0]).wait_recv()
        reduce2(1)
        march(0)
        for s in range(1, STEPS):
            reduce3(s)
            if s + 1 < STEPS:
                reduce2(s + 1)
            march(s)

    @pl.when(jnp.logical_not(is_root))
    def _():
        reduce2(0)
        local_part(1)
        reduce1(1)
        reduce3(0)
        local_part(2)
        reduce1(2)
        reduce2(1)
        local_part(3)
        reduce1(3)
        reduce3(1)
        reduce2(2)
        reduce3(2)
        reduce2(3)
        reduce3(3)
        pass_on(0)
        pass_on(1)
        fill(0)
        pass_on(2)
        fill(1)
        fill(2)
        pass_on(3)
        fill(3)
        for s in range(STEPS):
            finish(s)

    out_ref[...] = full[...]

    @pl.when(me < n - 1)
    def _():
        for i in range(BACK):
            halo_copy(i).wait_send()

    for s in range(STEPS):
        hub = hubs[s]
        for copy in copies1(s):
            copy.wait_send()
        for copy in copies2(s):
            copy.wait_send()

        @pl.when(is_root)
        def _(s=s, hub=hub):
            if s < BACK:
                for copy in copies_x(s):
                    copy.wait_send()
            if hub != 0:
                copy7(s).wait_send()

        @pl.when(jnp.logical_not(is_root))
        def _(s=s):
            copy3(s).wait_send()

        @pl.when(me == hub)
        def _(s=s, hub=hub):
            rest = full.at[s, pl.ds(0, (n - 1 - hub) * thin)]
            to(other, rest, rest, s4.at[s], r4.at[s]).wait_send()
            if hub != 0:
                for copy in copies_for_root(s):
                    copy.wait_send()

        for peer, copy in [*copies5(s), *copies6(s)]:
            if hub == 0:
                sent = jnp.logical_or(is_root, peer != 0)
            else:
                sent = jnp.logical_and(
                    jnp.logical_not(is_root),
                    jnp.logical_and(peer != 0, jnp.logical_or(me == hub, peer != hub)))

            @pl.when(sent)
            def _(copy=copy):
                copy.wait_send()


def per_device(
    n, n_pts, history, incident, kernel_blocks, block_row, block_col, lag_offset, mode_kernel,
    self_inverse,
):
    lags, points, modes = history.shape
    entries, size = kernel_blocks.shape[0], kernel_blocks.shape[1]
    rows = self_inverse.shape[0]
    f32, bf16 = jnp.float32, jnp.bfloat16
    vmem = pl.BlockSpec(memory_space=pltpu.VMEM)
    hbm = pl.BlockSpec(memory_space=pltpu.HBM)
    chunks = 8
    dma = pltpu.SemaphoreType.DMA

    part, pair = pl.pallas_call(
        functools.partial(history_kernel, chunks),
        out_shape=(
            jax.ShapeDtypeStruct((STEPS, rows, modes), f32),
            jax.ShapeDtypeStruct((BACK, 2 * rows, points), bf16),
        ),
        in_specs=[hbm] * 6,
        out_specs=(vmem, vmem),
        scratch_shapes=[
            pltpu.VMEM((lags, rows, points), f32),
            pltpu.VMEM((lags, rows, points), f32),
            pltpu.VMEM((2 * rows, points), bf16),
            pltpu.SMEM((entries,), jnp.int32),
            pltpu.SMEM((entries,), jnp.int32),
            pltpu.SMEM((entries,), jnp.int32),
            pltpu.VMEM((entries, size, size), bf16),
            pltpu.VMEM((lags, points, modes), bf16),
            pltpu.VMEM((lags, modes), f32),
            dma((5,)), dma((chunks,)),
        ],
        compiler_params=pltpu.CompilerParams(vmem_limit_bytes=VMEM_BYTES),
    )(block_row, block_col, lag_offset, kernel_blocks, history, mode_kernel)

    group = 4 if n % 4 == 0 else 1
    groups = n // group
    wide, thin = rows // group, rows // n
    peers, tops, sides = max(group - 1, 1), max(groups - 1, 1), max(n_pts - 1, 1)
    return pl.pallas_call(
        functools.partial(march_kernel, n, group, groups, n_pts),
        out_shape=jax.ShapeDtypeStruct((STEPS, rows, modes), f32),
        in_specs=[vmem, vmem, hbm, vmem, vmem, vmem],
        out_specs=vmem,
        scratch_shapes=[
            pltpu.VMEM((BACK, points, modes), bf16),
            pltpu.VMEM((rows // size, 2 * size, size), bf16),
            pltpu.VMEM((STEPS, rows, modes), f32),
            pltpu.VMEM((STEPS, peers, wide, modes), f32),
            pltpu.VMEM((STEPS, wide, modes), f32),
            pltpu.VMEM((STEPS, tops, thin, modes), f32),
            pltpu.VMEM((STEPS, thin, modes), f32),
            pltpu.VMEM((STEPS, rows, modes), f32),
            pltpu.VMEM((BACK, 2 * rows, points), bf16),
            pltpu.VMEM((BACK, points, modes), bf16),
            pltpu.VMEM((STEPS, rows, modes), f32),
            dma((STEPS, peers)), dma((STEPS,)),
            dma((STEPS, tops)), dma((STEPS,)),
            dma((STEPS,)), dma((STEPS,)),
            dma((STEPS,)), dma((STEPS,)),
            dma((STEPS, tops)), dma((STEPS,)),
            dma((STEPS, peers)), dma((STEPS,)),
            dma((STEPS,)), dma((STEPS,)), dma((STEPS, tops + peers)),
            dma((BACK, sides)), dma((BACK,)),
            dma((BACK,)), dma((BACK,)),
        ],
        compiler_params=pltpu.CompilerParams(
            collective_id=0, has_side_effects=True, vmem_limit_bytes=VMEM_BYTES),
    )(part, pair, history, mode_kernel, incident, self_inverse)


def solution(mesh):
    return jax.shard_map(
        functools.partial(per_device, mesh.shape["lag"], mesh.shape["pts"]),
        mesh=mesh,
        in_specs=(
            P("lag", None, None),
            P(None, "pts", None),
            P(("lag", "pts"), None, None),
            P(("lag", "pts")),
            P(("lag", "pts")),
            P(("lag", "pts")),
            P("lag", None),
            P("pts", None),
        ),
        out_specs=P(None, "pts", None),
        check_vma=False,
    )
```

time: 59.8 us -> 56.9 us (0.952)
  Pallas kernels: 49.1 us -> 54.9 us
  starting transfers between devices: 4.51 us -> 0 us
  local copies, waits for them, and re-layouts: 5.73 us -> 1.87 us
    pallas_call x1, Pallas kernels: 40.8 us -> 49.1 us  [per_device(): pl.pallas_call(functools.partial(march_kernel, n, group, groups, n_pts),...]
    ppermute x1 -> x0, starting transfers between devices: 4.51 us -> none  [per_device(): lax.ppermute(history[lags - BACK:], 'lag', [(i, i + 1) for i in range(n -...]
    unnamed x15 -> x1, local copies, waits for them, and re-layouts: 4.65 us -> 1.87 us
    pallas_call x1, Pallas kernels: 8.29 us -> 5.81 us  [per_device(): pl.pallas_call(functools.partial(history_kernel, chunks), out_shape=(jax....]
    slice x1 -> x0, local copies, waits for them, and re-layouts: 1.07 us -> none  [per_device(): history[lags - BACK:]]
  transfers between devices with their start and end apart: 1 -> 0, of which waited for: 0 -> 0; matrix products, arithmetic and copies ran while one was open for 0% -> 0% of each run, Pallas kernels for 14% -> 0%
where the time goes in v2:
time: 56.9 us; the launch traced here: 56.8 us
  Pallas kernels  54.9 us (96%)
  local copies, waits for them, and re-layouts  1.87 us (3%)
    pallas_call x1, Pallas kernels, per_device(): pl.pallas_call(functools.partial(march_kernel, n, group, groups, n_pts),...  49.1 us
    pallas_call x1, Pallas kernels, per_device(): pl.pallas_call(functools.partial(history_kernel, chunks), out_shape=(jax....  5.81 us
    unnamed x1, local copies, waits for them, and re-layouts  1.87 us

profile of v2, /device:TPU:1, one launch (start us, length us, event | category | flops | bytes accessed | tf_op | source)
XLA Modules:
  0.0 56.8 jit_solution(13829452734011295734)
XLA Ops:
  0.0 5.8 %shard_map.82 = (f32[4,256,128]{2,1,0:T(8,128)}, bf16[3,512,512]{2,1,0:T(8,128)(2,1)}) custom-call(s32[192]{0:T(256)} %row_hbm.1, s32[192]{0:T(256)} %col_hbm.1, s32[192]{0:T(256)} %lag_hbm.1, bf16[192,128,128]{2,1,0:T(8,128)(2,1)} %k_hbm.1, bf16[6,512,128]{2,1,0:T(8,128)(2,1)} %hist_hbm.3, f32[6,128]{1,0:T(8,128)} %mk_ref.1), custom_call_target="tpu_custom_call" | custom-call | tf_op jit(solution)/shard_map/pallas_call | solution.py:455
  5.8 49.1 %shard_map.83 = f32[4,256,128]{2,1,0:T(8,128)} custom-call(f32[4,256,128]{2,1,0:T(8,128)} %get-tuple-element.7.part_ref, bf16[3,512,512]{2,1,0:T(8,128)(2,1)} %get-tuple-element.8.pair_ref, bf16[6,512,128]{2,1,0:T(8,128)(2,1)} %hist_hbm.3, f32[6,128]{1,0:T(8,128)} %mk_ref.1, bf16[4,256,128]{2,1,0:T(8,128)(2,1)} %inc_ref.1, f32[256,128]{1,0:T(8,128)} %inv_ref.1), custom_call_target="tpu_custom_call" | custom-call | tf_op jit(solution)/shard_map/pallas_call | solution.py:482
  54.9 1.9 %copy.10 = f32[4,256,128]{2,1,0:T(8,128)} copy(f32[4,256,128]{2,1,0:T(8,128)} %shard_map.83) | data formatting | bytes 1048576

commit v3 on v2

--- a/solution.py
+++ b/solution.py
@@ -9,7 +9,6 @@
 STEPS = 4
 BACK = STEPS - 1
 MESH = pl.DeviceIdType.MESH
-VMEM_BYTES = 56 * 1024 * 1024
 
 
 def split_dot(pair, x):
@@ -86,25 +85,32 @@
 
 
 def march_kernel(
-    n, group, groups, n_pts,
+    n, n_pts,
     part_ref, pair_ref, hist_hbm, mk_ref, inc_ref, inv_ref, out_ref,
-    halo_ref, inv_pair, field, got1, sum1, got2, sum2, root_field, solved_pair, slabs, full,
-    s1, r1, s2, r2, s3, r3, s4, r4, s5, r5, s6, r6, s7, r7, s8, sx, rx, sh, rh,
+    halo_ref, inv_pair, field, got_c, sum_c, got_x, sum_x, got_z, sum_z,
+    root_field, solved_pair, slabs, full,
+    sc, rc, sw, rw, s2, r2, s3, r3, s4, r4, s5, r5, s6, r6, s7, r7, s8, s9, r9, sx, rx, sh, rh,
 ):
     me = lax.axis_index("lag")
     mine = lax.axis_index("pts")
-    g = lax.rem(me, group)
-    z = me // group
+    core = lax.rem(me, 2)
+    side = lax.rem(me // 2, 2)
+    z = me // 4
+    groups = n // 4
+    quarter = core * 2 + side
+    sibling = {"lag": me + 1 - 2 * core}
+    across = {"lag": me + 2 - 4 * side}
     rows = part_ref.shape[1]
     modes = part_ref.shape[2]
     points = halo_ref.shape[1]
     size = inv_ref.shape[1]
     row_blocks = rows // size
-    wide = rows // group
+    half = rows // 2
+    wide = rows // 4
     thin = rows // n
     is_root = me == 0
     lags = hist_hbm.shape[0]
-    hubs = [1 if s < BACK and group > 1 else 0 for s in range(STEPS)]
+    hubs = [1 if s < BACK else 0 for s in range(STEPS)]
 
     barrier = pltpu.get_barrier_semaphore()
 
@@ -127,9 +133,6 @@
             device_id=device, device_id_type=MESH,
         )
 
-    def in_group(k):
-        return lax.rem(g + k, group)
-
     def in_column(k):
         return lax.rem(z + k, groups)
 
@@ -138,22 +141,22 @@
 
     other = {"lag": lax.rem(me + 1, n)}
 
-    def copies1(s):
-        for k in range(1, group):
-            peer = in_group(k)
-            yield to({"lag": z * group + peer}, field.at[s, span(peer, wide)],
-                     got1.at[s, k - 1], s1.at[s, k - 1], r1.at[s])
+    def copy_c(s):
+        return to(sibling, field.at[s, span(1 - core, half)], got_c.at[s], sc.at[s], rc.at[s])
+
+    def copy_w(s):
+        return to(across, sum_c.at[s, span(1 - side, wide)], got_x.at[s], sw.at[s], rw.at[s])
 
     def copies2(s):
         for k in range(1, groups):
             peer = in_column(k)
-            yield to({"lag": peer * group + g}, sum1.at[s, span(peer, thin)],
-                     got2.at[s, k - 1], s2.at[s, k - 1], r2.at[s])
-
-    share = span(g * groups + z, thin)
+            yield to({"lag": peer * 4 + lax.rem(me, 4)}, sum_x.at[s, span(peer, thin)],
+                     got_z.at[s, k - 1], s2.at[s, k - 1], r2.at[s])
+
+    share = span(quarter * groups + z, thin)
 
     def copy3(s):
-        return to({"lag": 0}, sum2.at[s], root_field.at[s, share], s3.at[s], r3.at[s])
+        return to({"lag": 0}, sum_z.at[s], root_field.at[s, share], s3.at[s], r3.at[s])
 
     def halo_copy(i):
         return to({"lag": lax.rem(me + 1, n)}, hist_hbm.at[lags - BACK + i], halo_ref.at[i],
@@ -166,24 +169,25 @@
             total += mk_ref[l:l + 1, :] * split_dot(pair_ref[l], halo_ref[BACK + l - s])
         field[s] = total
 
-    def reduce1(s):
-        for copy in copies1(s):
-            copy.start()
-
-    def reduce2(s):
-        to(other, got1.at[s], got1.at[s], s1.at[s, 0], r1.at[s]).wait_recv()
-        total = field[s, span(g, wide), :]
-        for k in range(group - 1):
-            total += got1[s, k]
-        sum1[s] = total
+    def reduce_c(s):
+        copy_c(s).start()
+
+    def reduce_x(s):
+        copy_c(s).wait_recv()
+        sum_c[s] = field[s, span(core, half), :] + got_c[s]
+        copy_w(s).start()
+
+    def reduce_z(s):
+        copy_w(s).wait_recv()
+        sum_x[s] = sum_c[s, span(side, wide), :] + got_x[s]
         for copy in copies2(s):
             copy.start()
 
     def reduce3(s):
-        to(other, got2.at[s], got2.at[s], s2.at[s, 0], r2.at[s]).wait_recv()
-        total = sum1[s, span(z, thin), :]
+        to(other, got_z.at[s], got_z.at[s], s2.at[s, 0], r2.at[s]).wait_recv()
+        total = sum_x[s, span(z, thin), :]
         for k in range(groups - 1):
-            total += got2[s, k]
+            total += got_z[s, k]
 
         @pl.when(is_root)
         def _():
@@ -191,7 +195,7 @@
 
         @pl.when(jnp.logical_not(is_root))
         def _():
-            sum2[s] = total
+            sum_z[s] = total
             copy3(s).start()
 
     def solve(head, rest, r):
@@ -213,28 +217,30 @@
             yield to({"pts": lax.rem(mine + k, n_pts)}, here, here, sx.at[s, k - 1], rx.at[s])
 
     def copy4(s, j):
-        part = span(lax.rem(j, group) * groups + j // group, thin)
+        owner = lax.rem(j, 2) * 2 + lax.rem(j // 2, 2)
+        part = span(owner * groups + j // 4, thin)
         return to({"lag": j}, full.at[s, part], full.at[s, part], s4.at[s], r4.at[s])
 
     def copies5(s):
         for k in range(1, groups):
-            peer = in_column(k) * group + g
+            peer = in_column(k) * 4 + lax.rem(me, 4)
             here = full.at[s, share]
             yield peer, to({"lag": peer}, here, here, s5.at[s, k - 1], r5.at[s])
 
-    def copies6(s):
-        for k in range(1, group):
-            peer = z * group + in_group(k)
-            here = full.at[s, span(g, wide)]
-            yield peer, to({"lag": peer}, here, here, s6.at[s, k - 1], r6.at[s])
+    def copy6(s):
+        here = full.at[s, span(quarter, wide)]
+        return to(across, here, here, s6.at[s], r6.at[s])
+
+    def copy9(s):
+        here = full.at[s, span(core, half)]
+        return to(sibling, here, here, s9.at[s], r9.at[s])
 
     def copies_for_root(s):
         here = full.at[s, pl.ds(0, thin)]
         for k in range(1, groups):
-            yield to({"lag": k * group}, here, here, s8.at[s, k - 1], r5.at[s])
+            yield to({"lag": k * 4}, here, here, s8.at[s, k - 1], r5.at[s])
         here = full.at[s, pl.ds(0, wide)]
-        for k in range(2, group):
-            yield to({"lag": k}, here, here, s8.at[s, groups + k - 3], r6.at[s])
+        yield to({"lag": 2}, here, here, s8.at[s, groups - 1], r6.at[s])
 
     def copy7(s):
         return to({"lag": hubs[s]}, full.at[s], full.at[s], s7.at[s], r7.at[s])
@@ -248,18 +254,16 @@
         hub = hubs[s]
 
         def hand(j, carry):
-            copy4(s, j).start()
+            copy4(s, n + hub - j).start()
             return carry
 
         lax.fori_loop(hub + 1, n, hand, 0)
-        for peer, copy in [*copies5(s), *copies6(s)]:
-            if hub == 0:
-                copy.start()
-            else:
-                @pl.when(peer != 0)
-                def _(copy=copy):
-                    copy.start()
-        if hub != 0:
+        for unused, copy in copies5(s):
+            copy.start()
+        copy6(s).start()
+        if hub == 0:
+            copy9(s).start()
+        else:
             for copy in copies_for_root(s):
                 copy.start()
 
@@ -304,29 +308,35 @@
 
             pl.when(me != hubs[s])(plain)
 
-    def fill(s):
-        def plain():
+    def unless_hub(s, act):
+        if hubs[s] == 0:
+            act()
+        else:
+            pl.when(me != hubs[s])(act)
+
+    def fill_x(s):
+        def act():
             away = full.at[s, pl.ds(0, (groups - 1) * thin)]
             to(other, away, away, s5.at[s, 0], r5.at[s]).wait_recv()
-            for peer, copy in copies6(s):
-                @pl.when(needs(s, peer))
-                def _(copy=copy):
-                    copy.start()
-
-        if hubs[s] == 0:
-            plain()
-        else:
-            pl.when(me != hubs[s])(plain)
+
+            @pl.when(needs(s, across["lag"]))
+            def _():
+                copy6(s).start()
+
+        unless_hub(s, act)
+
+    def fill_c(s):
+        def act():
+            copy6(s).wait_recv()
+
+            @pl.when(needs(s, sibling["lag"]))
+            def _():
+                copy9(s).start()
+
+        unless_hub(s, act)
 
     def finish(s):
-        def plain():
-            away = full.at[s, pl.ds(0, (group - 1) * wide)]
-            to(other, away, away, s6.at[s, 0], r6.at[s]).wait_recv()
-
-        if hubs[s] == 0:
-            plain()
-        else:
-            pl.when(me != hubs[s])(plain)
+        unless_hub(s, lambda: copy9(s).wait_recv())
 
     field[0] = part_ref[0]
 
@@ -340,55 +350,74 @@
             inv_pair[r, size:, :] = rest
 
     pl.semaphore_wait(barrier, n + n_pts - 2)
-    reduce1(0)
-
-    @pl.when(me < n - 1)
-    def _():
-        for i in range(BACK - 1, -1, -1):
-            halo_copy(i).start()
+    reduce_c(0)
+
+    def send_halo():
+        @pl.when(me < n - 1)
+        def _():
+            for i in range(BACK - 1, -1, -1):
+                halo_copy(i).start()
 
     @pl.when(is_root)
     def _():
+        solve_pair(0)
+        reduce_x(0)
+        send_halo()
         for s in range(1, STEPS):
-            reduce1(s)
-        for l in range(BACK):
-            solve_pair(l)
-        reduce2(0)
+            reduce_c(s)
+        reduce_z(0)
+        reduce_x(1)
         reduce3(0)
         rest = root_field.at[0, pl.ds(thin, rows - thin)]
         to(other, rest, rest, s3.at[0], r3.at[0]).wait_recv()
-        reduce2(1)
         march(0)
-        for s in range(1, STEPS):
-            reduce3(s)
-            if s + 1 < STEPS:
-                reduce2(s + 1)
-            march(s)
+        reduce_z(1)
+        reduce_x(2)
+        solve_pair(1)
+        reduce3(1)
+        reduce_z(2)
+        reduce_x(3)
+        march(1)
+        solve_pair(2)
+        reduce3(2)
+        reduce_z(3)
+        march(2)
+        reduce3(3)
+        march(3)
 
     @pl.when(jnp.logical_not(is_root))
     def _():
-        reduce2(0)
+        reduce_x(0)
+        send_halo()
+        reduce_z(0)
         local_part(1)
-        reduce1(1)
+        reduce_c(1)
         reduce3(0)
+        reduce_x(1)
         local_part(2)
-        reduce1(2)
-        reduce2(1)
+        reduce_c(2)
+        reduce_z(1)
+        reduce_x(2)
         local_part(3)
-        reduce1(3)
+        reduce_c(3)
         reduce3(1)
-        reduce2(2)
+        reduce_z(2)
+        reduce_x(3)
         reduce3(2)
-        reduce2(3)
+        reduce_z(3)
         reduce3(3)
         pass_on(0)
         pass_on(1)
-        fill(0)
+        fill_x(0)
         pass_on(2)
-        fill(1)
-        fill(2)
+        fill_x(1)
+        fill_c(0)
+        fill_x(2)
+        fill_c(1)
+        fill_c(2)
         pass_on(3)
-        fill(3)
+        fill_x(3)
+        fill_c(3)
         for s in range(STEPS):
             finish(s)
 
@@ -401,8 +430,8 @@
 
     for s in range(STEPS):
         hub = hubs[s]
-        for copy in copies1(s):
-            copy.wait_send()
+        copy_c(s).wait_send()
+        copy_w(s).wait_send()
         for copy in copies2(s):
             copy.wait_send()
 
@@ -426,7 +455,14 @@
                 for copy in copies_for_root(s):
                     copy.wait_send()
 
-        for peer, copy in [*copies5(s), *copies6(s)]:
+        chain = [(across["lag"], copy6(s))]
+        if hub == 0:
+            chain.append((sibling["lag"], copy9(s)))
+        else:
+            @pl.when(jnp.logical_and(me > hub, needs(s, sibling["lag"])))
+            def _(s=s):
+                copy9(s).wait_send()
+        for peer, copy in [*copies5(s), *chain]:
             if hub == 0:
                 sent = jnp.logical_or(is_root, peer != 0)
             else:
@@ -450,6 +486,9 @@
     vmem = pl.BlockSpec(memory_space=pltpu.VMEM)
     hbm = pl.BlockSpec(memory_space=pltpu.HBM)
     chunks = 8
+    history_bytes = 6 * 1024 * 1024 + (
+        8 * lags * rows * points + 2 * entries * size * size + 2 * lags * points * modes
+        + 4 * (BACK + 1) * rows * points)
     dma = pltpu.SemaphoreType.DMA
 
     part, pair = pl.pallas_call(
@@ -472,15 +511,15 @@
             pltpu.VMEM((lags, modes), f32),
             dma((5,)), dma((chunks,)),
         ],
-        compiler_params=pltpu.CompilerParams(vmem_limit_bytes=VMEM_BYTES),
+        compiler_params=pltpu.CompilerParams(vmem_limit_bytes=history_bytes),
     )(block_row, block_col, lag_offset, kernel_blocks, history, mode_kernel)
 
-    group = 4 if n % 4 == 0 else 1
-    groups = n // group
-    wide, thin = rows // group, rows // n
-    peers, tops, sides = max(group - 1, 1), max(groups - 1, 1), max(n_pts - 1, 1)
+    groups = n // 4
+    wide, thin = rows // 4, rows // n
+    march_bytes = 8 * 1024 * 1024 + 40 * BACK * rows * points
+    tops, sides = max(groups - 1, 1), max(n_pts - 1, 1)
     return pl.pallas_call(
-        functools.partial(march_kernel, n, group, groups, n_pts),
+        functools.partial(march_kernel, n, n_pts),
         out_shape=jax.ShapeDtypeStruct((STEPS, rows, modes), f32),
         in_specs=[vmem, vmem, hbm, vmem, vmem, vmem],
         out_specs=vmem,
@@ -488,7 +527,9 @@
             pltpu.VMEM((BACK, points, modes), bf16),
             pltpu.VMEM((rows // size, 2 * size, size), bf16),
             pltpu.VMEM((STEPS, rows, modes), f32),
-            pltpu.VMEM((STEPS, peers, wide, modes), f32),
+            pltpu.VMEM((STEPS, rows // 2, modes), f32),
+            pltpu.VMEM((STEPS, rows // 2, modes), f32),
+            pltpu.VMEM((STEPS, wide, modes), f32),
             pltpu.VMEM((STEPS, wide, modes), f32),
             pltpu.VMEM((STEPS, tops, thin, modes), f32),
             pltpu.VMEM((STEPS, thin, modes), f32),
@@ -496,18 +537,15 @@
             pltpu.VMEM((BACK, 2 * rows, points), bf16),
             pltpu.VMEM((BACK, points, modes), bf16),
             pltpu.VMEM((STEPS, rows, modes), f32),
-            dma((STEPS, peers)), dma((STEPS,)),
-            dma((STEPS, tops)), dma((STEPS,)),
-            dma((STEPS,)), dma((STEPS,)),
-            dma((STEPS,)), dma((STEPS,)),
-            dma((STEPS, tops)), dma((STEPS,)),
-            dma((STEPS, peers)), dma((STEPS,)),
-            dma((STEPS,)), dma((STEPS,)), dma((STEPS, tops + peers)),
-            dma((BACK, sides)), dma((BACK,)),
-            dma((BACK,)), dma((BACK,)),
+            dma((STEPS,)), dma((STEPS,)), dma((STEPS,)), dma((STEPS,)),
+            dma((STEPS, tops)), dma((STEPS,)), dma((STEPS,)), dma((STEPS,)),
+            dma((STEPS,)), dma((STEPS,)), dma((STEPS, tops)), dma((STEPS,)),
+            dma((STEPS,)), dma((STEPS,)), dma((STEPS,)), dma((STEPS,)),
+            dma((STEPS, tops + 1)), dma((STEPS,)), dma((STEPS,)),
+            dma((BACK, sides)), dma((BACK,)), dma((BACK,)), dma((BACK,)),
         ],
         compiler_params=pltpu.CompilerParams(
-            collective_id=0, has_side_effects=True, vmem_limit_bytes=VMEM_BYTES),
+            collective_id=0, has_side_effects=True, vmem_limit_bytes=march_bytes),
     )(part, pair, history, mode_kernel, incident, self_inverse)
 
 

time: 56.9 us -> 60.3 us (1.060)
  the two profiles are of different devices: /device:TPU:1 before, /device:TPU:9 now
where the time goes in v3:
time: 60.3 us; the launch traced here: 60 us
  Pallas kernels  52.5 us (87%)
  local copies, waits for them, and re-layouts  7.44 us (12%)
    pallas_call x1, Pallas kernels, per_device(): pl.pallas_call(functools.partial(march_kernel, n, n_pts), out_shape=jax.S...  47.7 us
    unnamed x17, local copies, waits for them, and re-layouts  7.44 us
    pallas_call x1, Pallas kernels, per_device(): pl.pallas_call(functools.partial(history_kernel, chunks), out_shape=(jax....  4.8 us

profile of v3, /device:TPU:9, one launch (start us, length us, event | category | flops | bytes accessed | tf_op | source)
XLA Modules:
  0.0 60.0 jit_solution(7203529000031658651)
XLA Ops:
  0.0 0.0 copy-start
  0.0 2.8 %copy-done = bf16[192,128,128]{2,1,0:T(8,128)(2,1)S(1)} copy-done((bf16[192,128,128]{2,1,0:T(8,128)(2,1)S(1)}, bf16[192,128,128]{2,1,0:T(8,128)(2,1)}, u32[]{:S(2)}) %copy-start) | copy-done | bytes 6291480
  2.8 0.0 copy-start.1
  2.8 1.1 %copy-done.1 = bf16[6,512,128]{2,1,0:T(8,128)(2,1)S(1)} copy-done((bf16[6,512,128]{2,1,0:T(8,128)(2,1)S(1)}, bf16[6,512,128]{2,1,0:T(8,128)(2,1)}, u32[]{:S(2)}) %copy-start.1) | copy-done | bytes 786456
  3.9 0.0 copy-start.4
  3.9 0.7 %copy-done.4 = f32[6,128]{1,0:T(8,128)S(1)} copy-done((f32[6,128]{1,0:T(8,128)S(1)}, f32[6,128]{1,0:T(8,128)}, u32[]{:S(2)}) %copy-start.4) | copy-done | bytes 3096
  4.6 0.0 copy-start.5
  4.6 0.7 %copy-done.5 = s32[192]{0:T(256)S(1)} copy-done((s32[192]{0:T(256)S(1)}, s32[192]{0:T(256)}, u32[]{:S(2)}) %copy-start.5) | copy-done | bytes 792
  5.3 0.0 copy-start.6
  5.3 0.7 %copy-done.6 = s32[192]{0:T(256)S(1)} copy-done((s32[192]{0:T(256)S(1)}, s32[192]{0:T(256)}, u32[]{:S(2)}) %copy-start.6) | copy-done | bytes 792
  6.0 0.0 copy-start.7
  6.0 0.7 %copy-done.7 = s32[192]{0:T(256)S(1)} copy-done((s32[192]{0:T(256)S(1)}, s32[192]{0:T(256)}, u32[]{:S(2)}) %copy-start.7) | copy-done | bytes 792
  6.6 0.0 copy-start.2
  6.6 0.0 copy-start.3
  6.6 4.8 %shard_map.82 = (f32[4,256,128]{2,1,0:T(8,128)S(1)}, bf16[3,512,512]{2,1,0:T(8,128)(2,1)S(1)}) custom-call(s32[192]{0:T(256)S(1)} %copy-done.5, s32[192]{0:T(256)S(1)} %copy-done.6, s32[192]{0:T(256)S(1)} %copy-done.7, bf16[192,128,128]{2,1,0:T(8,128)(2,1)S(1)} %copy-done, bf16[6,512,128]{2,1,0:T(8,128)(2,1)S(1)} %copy-done.1, f32[6,128]{1,0:T(8,128)S(1)} %copy-done.4), custom_call_target="tpu_custom_call" | custom-call | tf_op jit(solution)/shard_map/pallas_call | solution.py:494
  11.5 0.0 copy-done.2
  11.5 0.0 copy-done.3
  11.5 47.7 %shard_map.83 = f32[4,256,128]{2,1,0:T(8,128)S(1)} custom-call(f32[4,256,128]{2,1,0:T(8,128)S(1)} %get-tuple-element.7.part_ref, bf16[3,512,512]{2,1,0:T(8,128)(2,1)S(1)} %get-tuple-element.8.pair_ref, bf16[6,512,128]{2,1,0:T(8,128)(2,1)S(1)} %copy-done.1, f32[6,128]{1,0:T(8,128)S(1)} %copy-done.4, bf16[4,256,128]{2,1,0:T(8,128)(2,1)S(1)} %copy-done.2, ...), custom_call_target="tpu_custom_call" | custom-call | tf_op jit(solution)/shard_map/pallas_call | solution.py:521
  59.2 0.8 %copy.10 = f32[4,256,128]{2,1,0:T(8,128)} copy(f32[4,256,128]{2,1,0:T(8,128)S(1)} %shard_map.83) | data formatting | bytes 1048576
Async XLA Ops:
  0.0 2.8 %copy-start = (bf16[192,128,128]{2,1,0:T(8,128)(2,1)S(1)}, bf16[192,128,128]{2,1,0:T(8,128)(2,1)}, u32[]{:S(2)}) copy-start(bf16[192,128,128]{2,1,0:T(8,128)(2,1)} %k_hbm.1) | copy-start | bytes 18874372
  2.8 1.1 %copy-start.1 = (bf16[6,512,128]{2,1,0:T(8,128)(2,1)S(1)}, bf16[6,512,128]{2,1,0:T(8,128)(2,1)}, u32[]{:S(2)}) copy-start(bf16[6,512,128]{2,1,0:T(8,128)(2,1)} %hist_hbm.3) | copy-start | bytes 2359300
  3.9 0.7 %copy-start.4 = (f32[6,128]{1,0:T(8,128)S(1)}, f32[6,128]{1,0:T(8,128)}, u32[]{:S(2)}) copy-start(f32[6,128]{1,0:T(8,128)} %mk_ref.1) | copy-start | bytes 9220
  4.6 0.7 %copy-start.5 = (s32[192]{0:T(256)S(1)}, s32[192]{0:T(256)}, u32[]{:S(2)}) copy-start(s32[192]{0:T(256)} %row_hbm.1) | copy-start | bytes 2308
  5.3 0.7 %copy-start.6 = (s32[192]{0:T(256)S(1)}, s32[192]{0:T(256)}, u32[]{:S(2)}) copy-start(s32[192]{0:T(256)} %col_hbm.1) | copy-start | bytes 2308
  6.0 0.7 %copy-start.7 = (s32[192]{0:T(256)S(1)}, s32[192]{0:T(256)}, u32[]{:S(2)}) copy-start(s32[192]{0:T(256)} %lag_hbm.1) | copy-start | bytes 2308
  6.6 4.8 %copy-start.2 = (bf16[4,256,128]{2,1,0:T(8,128)(2,1)S(1)}, bf16[4,256,128]{2,1,0:T(8,128)(2,1)}, u32[]{:S(2)}) copy-start(bf16[4,256,128]{2,1,0:T(8,128)(2,1)} %inc_ref.1) | copy-start | bytes 786436
  6.6 4.8 %copy-start.3 = (f32[256,128]{1,0:T(8,128)S(1)}, f32[256,128]{1,0:T(8,128)}, u32[]{:S(2)}) copy-start(f32[256,128]{1,0:T(8,128)} %inv_ref.1) | copy-start | bytes 393220

commit v4 on v3

v4 whole, which is shorter than its diff:
```python
import functools
import jax
import jax.numpy as jnp
from jax import lax
from jax.experimental import pallas as pl
from jax.experimental.pallas import tpu as pltpu
from jax.sharding import PartitionSpec as P

STEPS = 4
BACK = STEPS - 1
HISTORY_BYTES = 50 * 1024 * 1024
MESH = pl.DeviceIdType.MESH


def split_dot(pair, x):
    both = jnp.dot(pair, x, preferred_element_type=jnp.float32)
    half = both.shape[0] // 2
    return both[:half] + both[half:]


def split_rows(value):
    head = value.astype(jnp.bfloat16)
    rest = (value - head.astype(jnp.float32)).astype(jnp.bfloat16)
    return head, rest


def history_kernel(
    chunks, row_hbm, col_hbm, lag_hbm, k_hbm, hist_hbm, mk_hbm, part_ref, pair_ref,
    even, odd, work, row_ref, col_ref, lag_ref, k_ref, hist_ref, mk_ref, sem, k_sem,
):
    lags, rows, points = even.shape
    entries, size = k_ref.shape[0], k_ref.shape[1]
    modes = hist_ref.shape[2]
    chunk = entries // chunks
    pairs = [(row_hbm, row_ref), (col_hbm, col_ref), (lag_hbm, lag_ref),
             (hist_hbm, hist_ref), (mk_hbm, mk_ref)]
    loads = [pltpu.make_async_copy(src, dst, sem.at[i]) for i, (src, dst) in enumerate(pairs)]

    def load_k(c):
        span = pl.ds(c * chunk, chunk)
        return pltpu.make_async_copy(k_hbm.at[span], k_ref.at[span], k_sem.at[c])

    for copy in loads[:3]:
        copy.start()
    for c in range(chunks):
        load_k(c).start()
    for copy in loads[3:]:
        copy.start()
    even[...] = jnp.zeros_like(even)
    odd[...] = jnp.zeros_like(odd)
    for copy in loads[:3]:
        copy.wait()

    def add(total, e):
        r = pl.multiple_of(row_ref[e] * size, size)
        c = pl.multiple_of(col_ref[e] * size, size)
        total[lag_ref[e], pl.ds(r, size), pl.ds(c, size)] += k_ref[e].astype(jnp.float32)

    def take(c, carry):
        load_k(c).wait()

        def body(j, carry):
            add(even, c * chunk + 2 * j)
            add(odd, c * chunk + 2 * j + 1)
            return carry

        return lax.fori_loop(0, chunk // 2, body, carry, unroll=2)

    lax.fori_loop(0, chunks, take, 0)
    for copy in loads[3:]:
        copy.wait()
    for l in range(lags):
        head, rest = split_rows(even[l] + odd[l])
        target = pair_ref.at[l] if l < BACK else work
        target[:rows, :] = head
        target[rows:, :] = rest
        count = min(l, BACK) + 1
        x = jnp.concatenate([hist_ref[l - s] for s in range(count)], axis=1)
        found = split_dot(target[...], x)
        for s in range(count):
            term = found[:, s * modes:(s + 1) * modes] * mk_ref[l:l + 1, :]
            if l == s:
                part_ref[s] = term
            else:
                part_ref[s] += term


def march_kernel(
    n, n_pts,
    part_ref, pair_ref, halo_ref, mk_ref, inc_ref, inv_ref, out_ref,
    inv_pair, field, got_c, sum_c, got_x, sum_x, got_z, sum_z,
    root_field, solved_pair, slabs, full,
    sc, rc, sw, rw, s2, r2, s3, r3, s4, r4, s5, r5, s6, r6, s7, r7, s8, s9, r9, sx, rx,
):
    me = lax.axis_index("lag")
    mine = lax.axis_index("pts")
    core = lax.rem(me, 2)
    side = lax.rem(me // 2, 2)
    z = me // 4
    groups = n // 4
    quarter = core * 2 + side
    sibling = {"lag": me + 1 - 2 * core}
    across = {"lag": me + 2 - 4 * side}
    rows = part_ref.shape[1]
    points = halo_ref.shape[1]
    size = inv_ref.shape[1]
    row_blocks = rows // size
    half = rows // 2
    wide = rows // 4
    thin = rows // n
    is_root = me == 0

    barrier = pltpu.get_barrier_semaphore()

    def loop(first, last, act):
        def body(i, carry):
            act(i)
            return carry

        lax.fori_loop(first, last, body, 0)

    def greet(k):
        pl.semaphore_signal(
            barrier, inc=1, device_id={"lag": lax.rem(me + k, n)}, device_id_type=MESH
        )

    loop(1, n, greet)
    for k in range(1, n_pts):
        pl.semaphore_signal(
            barrier, inc=1, device_id={"pts": lax.rem(mine + k, n_pts)}, device_id_type=MESH
        )

    def to(device, src, dst, send, recv):
        return pltpu.make_async_remote_copy(
            src_ref=src, dst_ref=dst, send_sem=send, recv_sem=recv,
            device_id=device, device_id_type=MESH,
        )

    def span(first, count):
        return pl.ds(pl.multiple_of(first * count, count), count)

    other = {"lag": lax.rem(me + 1, n)}
    share = span(quarter * groups + z, thin)

    def awaited(ref, send, recv):
        to(other, ref, ref, send, recv).wait_recv()

    def column(k):
        return lax.rem(z + k, groups)

    def copy_c(s):
        return to(sibling, field.at[s, span(1 - core, half)], got_c.at[s], sc.at[s], rc.at[s])

    def copy_x(s):
        return to(across, sum_c.at[s, span(1 - side, wide)], got_x.at[s], sw.at[s], rw.at[s])

    def copy_z(s, k):
        peer = column(k)
        return to({"lag": peer * 4 + lax.rem(me, 4)}, sum_x.at[s, span(peer, thin)],
                  got_z.at[s, k - 1], s2.at[s, k - 1], r2.at[s])

    def copy_root(s):
        return to({"lag": 0}, sum_z.at[s], root_field.at[s, share], s3.at[s], r3.at[s])

    def add_term(s, l):
        field[s] += mk_ref[pl.ds(l, 1), :] * split_dot(pair_ref[l], halo_ref[BACK + l - s])

    def reduce_c(s):
        field[s] = part_ref[s]

        @pl.when(jnp.logical_not(is_root))
        def _():
            loop(0, s, lambda l: add_term(s, l))

        copy_c(s).start()

    def reduce_x(s):
        copy_c(s).wait_recv()
        sum_c[s] = field[s, span(core, half), :] + got_c[s]
        copy_x(s).start()

    def reduce_z(s):
        copy_x(s).wait_recv()
        sum_x[s] = sum_c[s, span(side, wide), :] + got_x[s]
        for k in range(1, groups):
            copy_z(s, k).start()

    def reduce_root(s):
        awaited(got_z.at[s], s2.at[s, 0], r2.at[s])
        total = sum_x[s, span(z, thin), :]
        for k in range(groups - 1):
            total += got_z[s, k]

        @pl.when(is_root)
        def _():
            root_field[s, 0:thin, :] = total

        @pl.when(jnp.logical_not(is_root))
        def _():
            sum_z[s] = total
            copy_root(s).start()

    def solve(head, rest, r):
        both = jnp.dot(inv_pair[r], head, preferred_element_type=jnp.float32)
        last = jnp.dot(inv_pair[r, :size, :], rest, preferred_element_type=jnp.float32)
        return both[:size] + both[size:] + last

    def solve_pair(l):
        for r in range(row_blocks):
            block = slice(r * size, (r + 1) * size)
            below = slice(rows + r * size, rows + (r + 1) * size)
            head, rest = split_rows(solve(pair_ref[l, block, :], pair_ref[l, below, :], r))
            solved_pair[l, block, :] = head
            solved_pair[l, below, :] = rest

    def copy_pts(s, k):
        here = slabs.at[s, span(mine, rows)]
        return to({"pts": lax.rem(mine + k, n_pts)}, here, here, sx.at[s, k - 1], rx.at[s])

    def copy4(s, j):
        owner = lax.rem(j, 2) * 2 + lax.rem(j // 2, 2)
        part = full.at[s, span(owner * groups + j // 4, thin)]
        return to({"lag": j}, part, part, s4.at[s], r4.at[s])

    def copy5(s, k):
        here = full.at[s, share]
        return to({"lag": column(k) * 4 + lax.rem(me, 4)}, here, here, s5.at[s, k - 1], r5.at[s])

    def copy6(s):
        here = full.at[s, span(quarter, wide)]
        return to(across, here, here, s6.at[s], r6.at[s])

    def copy7(s):
        return to({"lag": 1}, full.at[s], full.at[s], s7.at[s], r7.at[s])

    def copy8(s, k):
        here = full.at[s, pl.ds(0, thin)]
        return to({"lag": k * 4}, here, here, s8.at[s, k - 1], r5.at[s])

    def copy8_x(s):
        here = full.at[s, pl.ds(0, wide)]
        return to({"lag": 2}, here, here, s8.at[s, groups - 1], r6.at[s])

    def copy9(s):
        here = full.at[s, span(core, half)]
        return to(sibling, here, here, s9.at[s], r9.at[s])

    def take_away(s, l):
        @pl.when(l == 0)
        def _():
            awaited(slabs.at[s - 1, pl.ds(0, points - rows)], sx.at[s - 1, 0], rx.at[s - 1])

        full[s] -= mk_ref[pl.ds(l, 1), :] * split_dot(solved_pair[l], slabs[s - 1 - l])

    def march(s):
        awaited(root_field.at[s, pl.ds(thin, rows - thin)], s3.at[s], r3.at[s])
        for r in range(row_blocks):
            block = slice(r * size, (r + 1) * size)
            net = inc_ref[s, block, :].astype(jnp.float32) - root_field[s, block, :]
            full[s, block, :] = solve(*split_rows(net), r)
        loop(0, s, lambda i: take_away(s, s - 1 - i))

        @pl.when(s < BACK)
        def _():
            slabs[s, span(mine, rows), :] = full[s].astype(jnp.bfloat16)
            for k in range(1, n_pts):
                copy_pts(s, k).start()
            copy7(s).start()
            solve_pair(s)

    def hub_of(s):
        return jnp.where(s < BACK, 1, 0)

    def needs(s, peer):
        return jnp.logical_and(peer != 0, peer != hub_of(s))

    def hand_out(s):
        hub = hub_of(s)

        @pl.when(s < BACK)
        def _():
            copy7(s).wait_recv()
            for k in range(1, groups):
                copy8(s, k).start()
            copy8_x(s).start()

        loop(hub + 1, n, lambda j: copy4(s, n + hub - j).start())
        for k in range(1, groups):
            copy5(s, k).start()
        copy6(s).start()

        @pl.when(s == BACK)
        def _():
            copy9(s).start()

    def relays(s):
        return jnp.logical_and(jnp.logical_not(is_root), me != hub_of(s))

    def pass_on(s):
        pl.when(me == hub_of(s))(lambda: hand_out(s))

        @pl.when(relays(s))
        def _():
            awaited(full.at[s, share], s4.at[s], r4.at[s])
            for k in range(1, groups):
                pl.when(needs(s, column(k) * 4 + lax.rem(me, 4)))(
                    lambda copy=copy5(s, k): copy.start())

    def fill_x(s):
        @pl.when(relays(s))
        def _():
            awaited(full.at[s, pl.ds(0, (groups - 1) * thin)], s5.at[s, 0], r5.at[s])
            pl.when(needs(s, across["lag"]))(lambda: copy6(s).start())

    def fill_c(s):
        @pl.when(relays(s))
        def _():
            copy6(s).wait_recv()
            pl.when(needs(s, sibling["lag"]))(lambda: copy9(s).start())

    def finish(s):
        pl.when(relays(s))(lambda: copy9(s).wait_recv())

    @pl.when(is_root)
    def _():
        for r in range(row_blocks):
            head, rest = split_rows(inv_ref[r * size:(r + 1) * size, :])
            inv_pair[r, :size, :] = head
            inv_pair[r, size:, :] = rest

    pl.semaphore_wait(barrier, n + n_pts - 2)

    def within(s, act):
        pl.when(jnp.logical_and(s >= 0, s < STEPS))(lambda: act(s))

    def reduce_wave(t):
        within(t, reduce_c)
        within(t - 1, reduce_x)
        within(t - 2, reduce_z)
        within(t - 3, reduce_root)
        pl.when(jnp.logical_and(is_root, t >= 3))(lambda: march(t - 3))

    loop(0, STEPS + 3, reduce_wave)

    def spread_wave(t):
        within(t, pass_on)
        within(t - 1, fill_x)
        within(t - 2, fill_c)

    loop(0, STEPS + 2, spread_wave)
    loop(0, STEPS, finish)

    out_ref[...] = full[...]

    def drain(s):
        copy_c(s).wait_send()
        copy_x(s).wait_send()
        for k in range(1, groups):
            copy_z(s, k).wait_send()
        hub = hub_of(s)

        @pl.when(jnp.logical_and(is_root, s < BACK))
        def _():
            for k in range(1, n_pts):
                copy_pts(s, k).wait_send()
            copy7(s).wait_send()

        pl.when(jnp.logical_not(is_root))(lambda: copy_root(s).wait_send())

        @pl.when(me == hub)
        def _():
            loop(hub + 1, n, lambda j: copy4(s, j).wait_send())

        @pl.when(jnp.logical_and(me == hub, s < BACK))
        def _():
            for k in range(1, groups):
                copy8(s, k).wait_send()
            copy8_x(s).wait_send()

        gives = jnp.logical_or(me == hub, jnp.logical_not(is_root))

        def sent(peer):
            return jnp.logical_and(gives, jnp.logical_or(me == hub, needs(s, peer)))

        for k in range(1, groups):
            pl.when(sent(column(k) * 4 + lax.rem(me, 4)))(
                lambda copy=copy5(s, k): copy.wait_send())
        pl.when(sent(across["lag"]))(lambda: copy6(s).wait_send())
        to_sibling = jnp.where(s < BACK, me > 1, jnp.logical_or(is_root, sibling["lag"] != 0))
        pl.when(to_sibling)(lambda: copy9(s).wait_send())

    loop(0, STEPS, drain)


def per_device(
    n, n_pts, history, incident, kernel_blocks, block_row, block_col, lag_offset, mode_kernel,
    self_inverse,
):
    lags, points, modes = history.shape
    entries, size = kernel_blocks.shape[0], kernel_blocks.shape[1]
    rows = self_inverse.shape[0]
    f32, bf16 = jnp.float32, jnp.bfloat16
    vmem = pl.BlockSpec(memory_space=pltpu.VMEM)
    hbm = pl.BlockSpec(memory_space=pltpu.HBM)
    chunks = 8
    dma = pltpu.SemaphoreType.DMA

    halo = lax.ppermute(history[lags - BACK:], "lag", [(i, i + 1) for i in range(n - 1)])

    part, pair = pl.pallas_call(
        functools.partial(history_kernel, chunks),
        out_shape=(
            jax.ShapeDtypeStruct((STEPS, rows, modes), f32),
            jax.ShapeDtypeStruct((BACK, 2 * rows, points), bf16),
        ),
        in_specs=[hbm] * 6,
        out_specs=(vmem, vmem),
        scratch_shapes=[
            pltpu.VMEM((lags, rows, points), f32),
            pltpu.VMEM((lags, rows, points), f32),
            pltpu.VMEM((2 * rows, points), bf16),
            pltpu.SMEM((entries,), jnp.int32),
            pltpu.SMEM((entries,), jnp.int32),
            pltpu.SMEM((entries,), jnp.int32),
            pltpu.VMEM((entries, size, size), bf16),
            pltpu.VMEM((lags, points, modes), bf16),
            pltpu.VMEM((lags, modes), f32),
            dma((5,)), dma((chunks,)),
        ],
        compiler_params=pltpu.CompilerParams(vmem_limit_bytes=HISTORY_BYTES),
    )(block_row, block_col, lag_offset, kernel_blocks, history, mode_kernel)

    groups = n // 4
    wide, thin = rows // 4, rows // n
    march_bytes = 8 * 1024 * 1024 + 40 * BACK * rows * points
    tops, sides = max(groups - 1, 1), max(n_pts - 1, 1)
    return pl.pallas_call(
        functools.partial(march_kernel, n, n_pts),
        out_shape=jax.ShapeDtypeStruct((STEPS, rows, modes), f32),
        in_specs=[vmem] * 6,
        out_specs=vmem,
        scratch_shapes=[
            pltpu.VMEM((rows // size, 2 * size, size), bf16),
            pltpu.VMEM((STEPS, rows, modes), f32),
            pltpu.VMEM((STEPS, rows // 2, modes), f32),
            pltpu.VMEM((STEPS, rows // 2, modes), f32),
            pltpu.VMEM((STEPS, wide, modes), f32),
            pltpu.VMEM((STEPS, wide, modes), f32),
            pltpu.VMEM((STEPS, tops, thin, modes), f32),
            pltpu.VMEM((STEPS, thin, modes), f32),
            pltpu.VMEM((STEPS, rows, modes), f32),
            pltpu.VMEM((BACK, 2 * rows, points), bf16),
            pltpu.VMEM((BACK, points, modes), bf16),
            pltpu.VMEM((STEPS, rows, modes), f32),
            dma((STEPS,)), dma((STEPS,)), dma((STEPS,)), dma((STEPS,)),
            dma((STEPS, tops)), dma((STEPS,)), dma((STEPS,)), dma((STEPS,)),
            dma((STEPS,)), dma((STEPS,)), dma((STEPS, tops)), dma((STEPS,)),
            dma((STEPS,)), dma((STEPS,)), dma((STEPS,)), dma((STEPS,)),
            dma((STEPS, tops + 1)), dma((STEPS,)), dma((STEPS,)),
            dma((BACK, sides)), dma((BACK,)),
        ],
        compiler_params=pltpu.CompilerParams(
            collective_id=0, has_side_effects=True, vmem_limit_bytes=march_bytes),
    )(part, pair, halo, mode_kernel, incident, self_inverse)


def solution(mesh):
    return jax.shard_map(
        functools.partial(per_device, mesh.shape["lag"], mesh.shape["pts"]),
        mesh=mesh,
        in_specs=(
            P("lag", None, None),
            P(None, "pts", None),
            P(("lag", "pts"), None, None),
            P(("lag", "pts")),
            P(("lag", "pts")),
            P(("lag", "pts")),
            P("lag", None),
            P("pts", None),
        ),
        out_specs=P(None, "pts", None),
        check_vma=False,
    )
```

time: 60.3 us -> 55.5 us (0.920)
  Pallas kernels: 52.5 us -> 45.7 us
  starting transfers between devices: 0 us -> 3.68 us
  local copies, waits for them, and re-layouts: 7.44 us -> 5.73 us
    pallas_call x1, Pallas kernels: 47.7 us -> 40.7 us  [per_device(): pl.pallas_call(functools.partial(march_kernel, n, n_pts), out_shape=jax.S...]
    ppermute x0 -> x1, starting transfers between devices: none -> 3.68 us  [per_device(): lax.ppermute(history[lags - BACK:], 'lag', [(i, i + 1) for i in range(n -...]
    unnamed x17 -> x15, local copies, waits for them, and re-layouts: 7.44 us -> 4.65 us
    slice x0 -> x1, local copies, waits for them, and re-layouts: none -> 1.07 us  [per_device(): history[lags - BACK:]]
  transfers between devices with their start and end apart: 0 -> 1, of which waited for: 0 -> 0; matrix products, arithmetic and copies ran while one was open for 0% -> 0% of each run, Pallas kernels for 0% -> 9%
where the time goes in v4:
time: 55.5 us; the launch traced here: 55.2 us
  Pallas kernels  45.7 us (82%)
  local copies, waits for them, and re-layouts  5.73 us (10%)
  starting transfers between devices  3.68 us (7%)
    pallas_call x1, Pallas kernels, per_device(): pl.pallas_call(functools.partial(march_kernel, n, n_pts), out_shape=jax.S...  40.7 us
    pallas_call x1, Pallas kernels, per_device(): pl.pallas_call(functools.partial(history_kernel, chunks), out_shape=(jax....  5.02 us
    unnamed x15, local copies, waits for them, and re-layouts  4.65 us
    ppermute x1, starting transfers between devices, per_device(): lax.ppermute(history[lags - BACK:], 'lag', [(i, i + 1) for i in range(n -...  3.68 us
  transfers between devices with their start and end apart: 1, of which 0 were waited for; matrix products, arithmetic and copies ran while one was open for 0% of the time, Pallas kernels for 9%

profile of v4, /device:TPU:9, one launch (start us, length us, event | category | flops | bytes accessed | tf_op | source)
XLA Modules:
  0.0 55.2 jit_solution(15918048171904839761)
XLA Ops:
  0.0 0.0 copy-start.2
  0.0 0.0 copy-start.1
  0.0 1.1 %slice.3 = bf16[3,512,128]{2,1,0:T(8,128)(2,1)S(1)} slice(bf16[6,512,128]{2,1,0:T(8,128)(2,1)} %hist_hbm.1), slice={[3:6], [0:512], [0:128]} | slice | bytes 786432 | tf_op jit(solution)/shard_map/slice | solution.py:408
  1.1 3.7 %collective-permute-start = (bf16[3,512,128]{2,1,0:T(8,128)(2,1)S(1)}, bf16[3,512,128]{2,1,0:T(8,128)(2,1)S(1)}, u32[]{:S(2)}, u32[]{:S(2)}) collective-permute-start(bf16[3,512,128]{2,1,0:T(8,128)(2,1)S(1)} %slice.3), channel_id=1, source_target_pairs={{0,2},{2,4},{4,6},{6,8},{8,10},{10,12},{12,14},{14,16},{16,18},{18... | collective-permute-start | bytes 1179656 | tf_op jit(solution)/shard_map/ppermute | solution.py:408
  4.8 0.0 copy-start
  4.8 1.1 %copy-done = bf16[6,512,128]{2,1,0:T(8,128)(2,1)S(1)} copy-done((bf16[6,512,128]{2,1,0:T(8,128)(2,1)S(1)}, bf16[6,512,128]{2,1,0:T(8,128)(2,1)}, u32[]{:S(2)}) %copy-start) | copy-done | bytes 786456
  5.9 0.0 copy-start.3
  5.9 0.7 %copy-done.3 = f32[6,128]{1,0:T(8,128)S(1)} copy-done((f32[6,128]{1,0:T(8,128)S(1)}, f32[6,128]{1,0:T(8,128)}, u32[]{:S(2)}) %copy-start.3) | copy-done | bytes 3096
  6.6 0.0 copy-start.4
  6.6 0.7 %copy-done.4 = s32[192]{0:T(256)S(1)} copy-done((s32[192]{0:T(256)S(1)}, s32[192]{0:T(256)}, u32[]{:S(2)}) %copy-start.4) | copy-done | bytes 792
  7.3 0.0 copy-start.5
  7.3 0.7 %copy-done.5 = s32[192]{0:T(256)S(1)} copy-done((s32[192]{0:T(256)S(1)}, s32[192]{0:T(256)}, u32[]{:S(2)}) %copy-start.5) | copy-done | bytes 792
  8.0 0.0 copy-start.6
  8.0 0.7 %copy-done.6 = s32[192]{0:T(256)S(1)} copy-done((s32[192]{0:T(256)S(1)}, s32[192]{0:T(256)}, u32[]{:S(2)}) %copy-start.6) | copy-done | bytes 792
  8.6 5.0 %shard_map.82 = (f32[4,256,128]{2,1,0:T(8,128)S(1)}, bf16[3,512,512]{2,1,0:T(8,128)(2,1)S(1)}) custom-call(s32[192]{0:T(256)S(1)} %copy-done.4, s32[192]{0:T(256)S(1)} %copy-done.5, s32[192]{0:T(256)S(1)} %copy-done.6, bf16[192,128,128]{2,1,0:T(8,128)(2,1)} %k_hbm.1, bf16[6,512,128]{2,1,0:T(8,128)(2,1)S(1)} %copy-done, f32[6,128]{1,0:T(8,128)S(1)} %copy-done.3), custom_call_target="tpu_custom_call" | custom-call | tf_op jit(solution)/shard_map/pallas_call | solution.py:410
  13.7 0.0 collective-permute-done.halo_ref
  13.7 0.0 copy-done.2
  13.7 0.0 copy-done.1
  13.7 40.7 %shard_map.83 = f32[4,256,128]{2,1,0:T(8,128)S(1)} custom-call(f32[4,256,128]{2,1,0:T(8,128)S(1)} %get-tuple-element.7.part_ref, bf16[3,512,512]{2,1,0:T(8,128)(2,1)S(1)} %get-tuple-element.8.pair_ref, bf16[3,512,128]{2,1,0:T(8,128)(2,1)S(1)} %collective-permute-done.halo_ref, f32[6,128]{1,0:T(8,128)S(1)} %copy-done.3, bf16[4,256,128]{2,1,0:T(8,128)(2,1)S(1)} %copy-done.1, ...), custom_call_target="tpu_custom_call" | custom-call | tf_op jit(solution)/shard_map/pallas_call | solution.py:437
  54.4 0.8 %copy.10 = f32[4,256,128]{2,1,0:T(8,128)} copy(f32[4,256,128]{2,1,0:T(8,128)S(1)} %shard_map.83) | data formatting | bytes 1048576
Async XLA Ops:
  0.0 13.7 %copy-start.2 = (f32[256,128]{1,0:T(8,128)S(1)}, f32[256,128]{1,0:T(8,128)}, u32[]{:S(2)}) copy-start(f32[256,128]{1,0:T(8,128)} %inv_ref.1) | copy-start | bytes 393220
  0.0 13.7 %copy-start.1 = (bf16[4,256,128]{2,1,0:T(8,128)(2,1)S(1)}, bf16[4,256,128]{2,1,0:T(8,128)(2,1)}, u32[]{:S(2)}) copy-start(bf16[4,256,128]{2,1,0:T(8,128)(2,1)} %inc_ref.1) | copy-start | bytes 786436
  1.1 12.6 %collective-permute-start = (bf16[3,512,128]{2,1,0:T(8,128)(2,1)S(1)}, bf16[3,512,128]{2,1,0:T(8,128)(2,1)S(1)}, u32[]{:S(2)}, u32[]{:S(2)}) collective-permute-start(bf16[3,512,128]{2,1,0:T(8,128)(2,1)S(1)} %slice.3), channel_id=1, source_target_pairs={{0,2},{2,4},{4,6},{6,8},{8,10},{10,12},{12,14},{14,16},{16,18},{18... | collective-permute-start | bytes 1179656 | tf_op jit(solution)/shard_map/ppermute | solution.py:408
  4.8 1.1 %copy-start = (bf16[6,512,128]{2,1,0:T(8,128)(2,1)S(1)}, bf16[6,512,128]{2,1,0:T(8,128)(2,1)}, u32[]{:S(2)}) copy-start(bf16[6,512,128]{2,1,0:T(8,128)(2,1)} %hist_hbm.1) | copy-start | bytes 2359300
  5.9 0.7 %copy-start.3 = (f32[6,128]{1,0:T(8,128)S(1)}, f32[6,128]{1,0:T(8,128)}, u32[]{:S(2)}) copy-start(f32[6,128]{1,0:T(8,128)} %mk_ref.1) | copy-start | bytes 9220
  6.6 0.7 %copy-start.4 = (s32[192]{0:T(256)S(1)}, s32[192]{0:T(256)}, u32[]{:S(2)}) copy-start(s32[192]{0:T(256)} %row_hbm.1) | copy-start | bytes 2308
  7.3 0.7 %copy-start.5 = (s32[192]{0:T(256)S(1)}, s32[192]{0:T(256)}, u32[]{:S(2)}) copy-start(s32[192]{0:T(256)} %col_hbm.1) | copy-start | bytes 2308
  8.0 0.7 %copy-start.6 = (s32[192]{0:T(256)S(1)}, s32[192]{0:T(256)}, u32[]{:S(2)}) copy-start(s32[192]{0:T(256)} %lag_hbm.1) | copy-start | bytes 2308

commit v5 on v4

--- a/solution.py
+++ b/solution.py
@@ -8,7 +8,7 @@
 
 STEPS = 4
 BACK = STEPS - 1
-HISTORY_BYTES = 50 * 1024 * 1024
+HISTORY_BYTES = 54 * 1024 * 1024
 MESH = pl.DeviceIdType.MESH
 
 
@@ -88,24 +88,18 @@
 def march_kernel(
     n, n_pts,
     part_ref, pair_ref, halo_ref, mk_ref, inc_ref, inv_ref, out_ref,
-    inv_pair, field, got_c, sum_c, got_x, sum_x, got_z, sum_z,
-    root_field, solved_pair, slabs, full,
-    sc, rc, sw, rw, s2, r2, s3, r3, s4, r4, s5, r5, s6, r6, s7, r7, s8, s9, r9, sx, rx,
+    inv_pair, field, got, share_sum, root_field, solved_pair, slabs, full,
+    sa, ra, s3, r3, s4, r4, s5, r5, s6, r6, s7, r7, s8, sx, rx,
 ):
     me = lax.axis_index("lag")
     mine = lax.axis_index("pts")
-    core = lax.rem(me, 2)
-    side = lax.rem(me // 2, 2)
     z = me // 4
     groups = n // 4
-    quarter = core * 2 + side
-    sibling = {"lag": me + 1 - 2 * core}
-    across = {"lag": me + 2 - 4 * side}
+    quarter = lax.rem(me, 4)
     rows = part_ref.shape[1]
     points = halo_ref.shape[1]
     size = inv_ref.shape[1]
     row_blocks = rows // size
-    half = rows // 2
     wide = rows // 4
     thin = rows // n
     is_root = me == 0
@@ -140,7 +134,11 @@
         return pl.ds(pl.multiple_of(first * count, count), count)
 
     other = {"lag": lax.rem(me + 1, n)}
-    share = span(quarter * groups + z, thin)
+
+    def share_of(j):
+        return span(lax.rem(j, 4) * groups + j // 4, thin)
+
+    share = share_of(me)
 
     def awaited(ref, send, recv):
         to(other, ref, ref, send, recv).wait_recv()
@@ -148,48 +146,33 @@
     def column(k):
         return lax.rem(z + k, groups)
 
-    def copy_c(s):
-        return to(sibling, field.at[s, span(1 - core, half)], got_c.at[s], sc.at[s], rc.at[s])
-
-    def copy_x(s):
-        return to(across, sum_c.at[s, span(1 - side, wide)], got_x.at[s], sw.at[s], rw.at[s])
-
-    def copy_z(s, k):
-        peer = column(k)
-        return to({"lag": peer * 4 + lax.rem(me, 4)}, sum_x.at[s, span(peer, thin)],
-                  got_z.at[s, k - 1], s2.at[s, k - 1], r2.at[s])
+    def in_group(k):
+        return z * 4 + lax.rem(me + k, 4)
+
+    def copy_a(s, k):
+        peer = lax.rem(me + k, n)
+        return to({"lag": peer}, field.at[s, share_of(peer)], got.at[s, k - 1], sa.at[s], ra.at[s])
 
     def copy_root(s):
-        return to({"lag": 0}, sum_z.at[s], root_field.at[s, share], s3.at[s], r3.at[s])
+        return to({"lag": 0}, share_sum.at[s], root_field.at[s, share], s3.at[s], r3.at[s])
 
     def add_term(s, l):
         field[s] += mk_ref[pl.ds(l, 1), :] * split_dot(pair_ref[l], halo_ref[BACK + l - s])
 
-    def reduce_c(s):
+    def reduce_all(s):
         field[s] = part_ref[s]
 
         @pl.when(jnp.logical_not(is_root))
         def _():
             loop(0, s, lambda l: add_term(s, l))
 
-        copy_c(s).start()
-
-    def reduce_x(s):
-        copy_c(s).wait_recv()
-        sum_c[s] = field[s, span(core, half), :] + got_c[s]
-        copy_x(s).start()
-
-    def reduce_z(s):
-        copy_x(s).wait_recv()
-        sum_x[s] = sum_c[s, span(side, wide), :] + got_x[s]
-        for k in range(1, groups):
-            copy_z(s, k).start()
+        loop(1, n, lambda k: copy_a(s, k).start())
 
     def reduce_root(s):
-        awaited(got_z.at[s], s2.at[s, 0], r2.at[s])
-        total = sum_x[s, span(z, thin), :]
-        for k in range(groups - 1):
-            total += got_z[s, k]
+        awaited(got.at[s], sa.at[s], ra.at[s])
+        total = field[s, share, :]
+        for k in range(n - 1):
+            total += got[s, k]
 
         @pl.when(is_root)
         def _():
@@ -197,7 +180,7 @@
 
         @pl.when(jnp.logical_not(is_root))
         def _():
-            sum_z[s] = total
+            share_sum[s] = total
             copy_root(s).start()
 
     def solve(head, rest, r):
@@ -218,17 +201,16 @@
         return to({"pts": lax.rem(mine + k, n_pts)}, here, here, sx.at[s, k - 1], rx.at[s])
 
     def copy4(s, j):
-        owner = lax.rem(j, 2) * 2 + lax.rem(j // 2, 2)
-        part = full.at[s, span(owner * groups + j // 4, thin)]
+        part = full.at[s, share_of(j)]
         return to({"lag": j}, part, part, s4.at[s], r4.at[s])
 
     def copy5(s, k):
         here = full.at[s, share]
-        return to({"lag": column(k) * 4 + lax.rem(me, 4)}, here, here, s5.at[s, k - 1], r5.at[s])
-
-    def copy6(s):
+        return to({"lag": column(k) * 4 + quarter}, here, here, s5.at[s, k - 1], r5.at[s])
+
+    def copy6(s, k):
         here = full.at[s, span(quarter, wide)]
-        return to(across, here, here, s6.at[s], r6.at[s])
+        return to({"lag": in_group(k)}, here, here, s6.at[s, k - 1], r6.at[s])
 
     def copy7(s):
         return to({"lag": 1}, full.at[s], full.at[s], s7.at[s], r7.at[s])
@@ -237,13 +219,9 @@
         here = full.at[s, pl.ds(0, thin)]
         return to({"lag": k * 4}, here, here, s8.at[s, k - 1], r5.at[s])
 
-    def copy8_x(s):
+    def copy8_q(s, k):
         here = full.at[s, pl.ds(0, wide)]
-        return to({"lag": 2}, here, here, s8.at[s, groups - 1], r6.at[s])
-
-    def copy9(s):
-        here = full.at[s, span(core, half)]
-        return to(sibling, here, here, s9.at[s], r9.at[s])
+        return to({"lag": k}, here, here, s8.at[s, groups + k - 3], r6.at[s])
 
     def take_away(s, l):
         @pl.when(l == 0)
@@ -282,16 +260,15 @@
             copy7(s).wait_recv()
             for k in range(1, groups):
                 copy8(s, k).start()
-            copy8_x(s).start()
+            for k in range(2, 4):
+                copy8_q(s, k).start()
 
         loop(hub + 1, n, lambda j: copy4(s, n + hub - j).start())
         for k in range(1, groups):
             copy5(s, k).start()
-        copy6(s).start()
-
-        @pl.when(s == BACK)
-        def _():
-            copy9(s).start()
+        for k in range(1, 4):
+            pl.when(jnp.logical_or(is_root, in_group(k) != 0))(
+                lambda copy=copy6(s, k): copy.start())
 
     def relays(s):
         return jnp.logical_and(jnp.logical_not(is_root), me != hub_of(s))
@@ -303,23 +280,19 @@
         def _():
             awaited(full.at[s, share], s4.at[s], r4.at[s])
             for k in range(1, groups):
-                pl.when(needs(s, column(k) * 4 + lax.rem(me, 4)))(
+                pl.when(needs(s, column(k) * 4 + quarter))(
                     lambda copy=copy5(s, k): copy.start())
 
     def fill_x(s):
         @pl.when(relays(s))
         def _():
             awaited(full.at[s, pl.ds(0, (groups - 1) * thin)], s5.at[s, 0], r5.at[s])
-            pl.when(needs(s, across["lag"]))(lambda: copy6(s).start())
-
-    def fill_c(s):
-        @pl.when(relays(s))
-        def _():
-            copy6(s).wait_recv()
-            pl.when(needs(s, sibling["lag"]))(lambda: copy9(s).start())
+            for k in range(1, 4):
+                pl.when(needs(s, in_group(k)))(lambda copy=copy6(s, k): copy.start())
 
     def finish(s):
-        pl.when(relays(s))(lambda: copy9(s).wait_recv())
+        pl.when(relays(s))(
+            lambda: awaited(full.at[s, pl.ds(0, 3 * wide)], s6.at[s, 0], r6.at[s]))
 
     @pl.when(is_root)
     def _():
@@ -334,29 +307,24 @@
         pl.when(jnp.logical_and(s >= 0, s < STEPS))(lambda: act(s))
 
     def reduce_wave(t):
-        within(t, reduce_c)
-        within(t - 1, reduce_x)
-        within(t - 2, reduce_z)
-        within(t - 3, reduce_root)
-        pl.when(jnp.logical_and(is_root, t >= 3))(lambda: march(t - 3))
-
-    loop(0, STEPS + 3, reduce_wave)
+        within(t, reduce_all)
+        within(t - 1, reduce_root)
+        pl.when(jnp.logical_and(is_root, t >= 2))(lambda: march(t - 2))
+
+    loop(0, STEPS + 2, reduce_wave)
 
     def spread_wave(t):
         within(t, pass_on)
         within(t - 1, fill_x)
-        within(t - 2, fill_c)
-
-    loop(0, STEPS + 2, spread_wave)
+
+    loop(0, STEPS + 1, spread_wave)
     loop(0, STEPS, finish)
 
     out_ref[...] = full[...]
 
     def drain(s):
-        copy_c(s).wait_send()
-        copy_x(s).wait_send()
-        for k in range(1, groups):
-            copy_z(s, k).wait_send()
+        rest = field.at[s, pl.ds(0, rows - thin)]
+        to(other, rest, rest, sa.at[s], ra.at[s]).wait_send()
         hub = hub_of(s)
 
         @pl.when(jnp.logical_and(is_root, s < BACK))
@@ -375,7 +343,8 @@
         def _():
             for k in range(1, groups):
                 copy8(s, k).wait_send()
-            copy8_x(s).wait_send()
+            for k in range(2, 4):
+                copy8_q(s, k).wait_send()
 
         gives = jnp.logical_or(me == hub, jnp.logical_not(is_root))
 
@@ -383,11 +352,12 @@
             return jnp.logical_and(gives, jnp.logical_or(me == hub, needs(s, peer)))
 
         for k in range(1, groups):
-            pl.when(sent(column(k) * 4 + lax.rem(me, 4)))(
+            pl.when(sent(column(k) * 4 + quarter))(
                 lambda copy=copy5(s, k): copy.wait_send())
-        pl.when(sent(across["lag"]))(lambda: copy6(s).wait_send())
-        to_sibling = jnp.where(s < BACK, me > 1, jnp.logical_or(is_root, sibling["lag"] != 0))
-        pl.when(to_sibling)(lambda: copy9(s).wait_send())
+        for k in range(1, 4):
+            peer = in_group(k)
+            reached = jnp.where(me == hub, jnp.logical_or(is_root, peer != 0), sent(peer))
+            pl.when(reached)(lambda copy=copy6(s, k): copy.wait_send())
 
     loop(0, STEPS, drain)
 
@@ -431,7 +401,7 @@
     )(block_row, block_col, lag_offset, kernel_blocks, history, mode_kernel)
 
     groups = n // 4
-    wide, thin = rows // 4, rows // n
+    thin = rows // n
     march_bytes = 8 * 1024 * 1024 + 40 * BACK * rows * points
     tops, sides = max(groups - 1, 1), max(n_pts - 1, 1)
     return pl.pallas_call(
@@ -442,21 +412,16 @@
         scratch_shapes=[
             pltpu.VMEM((rows // size, 2 * size, size), bf16),
             pltpu.VMEM((STEPS, rows, modes), f32),
-            pltpu.VMEM((STEPS, rows // 2, modes), f32),
-            pltpu.VMEM((STEPS, rows // 2, modes), f32),
-            pltpu.VMEM((STEPS, wide, modes), f32),
-            pltpu.VMEM((STEPS, wide, modes), f32),
-            pltpu.VMEM((STEPS, tops, thin, modes), f32),
+            pltpu.VMEM((STEPS, n - 1, thin, modes), f32),
             pltpu.VMEM((STEPS, thin, modes), f32),
             pltpu.VMEM((STEPS, rows, modes), f32),
             pltpu.VMEM((BACK, 2 * rows, points), bf16),
             pltpu.VMEM((BACK, points, modes), bf16),
             pltpu.VMEM((STEPS, rows, modes), f32),
             dma((STEPS,)), dma((STEPS,)), dma((STEPS,)), dma((STEPS,)),
-            dma((STEPS, tops)), dma((STEPS,)), dma((STEPS,)), dma((STEPS,)),
             dma((STEPS,)), dma((STEPS,)), dma((STEPS, tops)), dma((STEPS,)),
-            dma((STEPS,)), dma((STEPS,)), dma((STEPS,)), dma((STEPS,)),
-            dma((STEPS, tops + 1)), dma((STEPS,)), dma((STEPS,)),
+            dma((STEPS, 3)), dma((STEPS,)), dma((STEPS,)), dma((STEPS,)),
+            dma((STEPS, tops + 2)),
             dma((BACK, sides)), dma((BACK,)),
         ],
         compiler_params=pltpu.CompilerParams(

time: 55.5 us -> 53.4 us (0.962)
  the two profiles are of different devices: /device:TPU:9 before, /device:TPU:1 now
where the time goes in v5:
time: 53.4 us; the launch traced here: 53.2 us
  Pallas kernels  44.3 us (83%)
  starting transfers between devices  4.51 us (8%)
  local copies, waits for them, and re-layouts  4.33 us (8%)
    pallas_call x1, Pallas kernels, per_device(): pl.pallas_call(functools.partial(march_kernel, n, n_pts), out_shape=jax.S...  38.5 us
    pallas_call x1, Pallas kernels, per_device(): pl.pallas_call(functools.partial(history_kernel, chunks), out_shape=(jax....  5.82 us
    ppermute x1, starting transfers between devices, per_device(): lax.ppermute(history[lags - BACK:], 'lag', [(i, i + 1) for i in range(n -...  4.51 us
    unnamed x11, local copies, waits for them, and re-layouts  3.25 us
    slice x1, local copies, waits for them, and re-layouts, per_device(): history[lags - BACK:]  1.08 us
  transfers between devices with their start and end apart: 1, of which 0 were waited for; matrix products, arithmetic and copies ran while one was open for 0% of the time, Pallas kernels for 11%

profile of v5, /device:TPU:1, one launch (start us, length us, event | category | flops | bytes accessed | tf_op | source)
XLA Modules:
  0.0 53.2 jit_solution(5129873592834283964)
XLA Ops:
  0.0 0.0 copy-start.4
  0.0 0.0 copy-start.3
  0.0 0.0 copy-start.2
  0.0 1.1 %slice.3 = bf16[3,512,128]{2,1,0:T(8,128)(2,1)S(1)} slice(bf16[6,512,128]{2,1,0:T(8,128)(2,1)} %hist_hbm.1), slice={[3:6], [0:512], [0:128]} | slice | bytes 786432 | tf_op jit(solution)/shard_map/slice | solution.py:378
  1.1 4.5 %collective-permute-start = (bf16[3,512,128]{2,1,0:T(8,128)(2,1)S(1)}, bf16[3,512,128]{2,1,0:T(8,128)(2,1)S(1)}, u32[]{:S(2)}, u32[]{:S(2)}) collective-permute-start(bf16[3,512,128]{2,1,0:T(8,128)(2,1)S(1)} %slice.3), channel_id=1, source_target_pairs={{0,2},{2,4},{4,6},{6,8},{8,10},{10,12},{12,14},{14,16},{16,18},{18... | collective-permute-start | bytes 1179656 | tf_op jit(solution)/shard_map/ppermute | solution.py:378
  5.6 5.8 %shard_map.82 = (f32[4,256,128]{2,1,0:T(8,128)}, bf16[3,512,512]{2,1,0:T(8,128)(2,1)}) custom-call(s32[192]{0:T(256)} %row_hbm.1, s32[192]{0:T(256)} %col_hbm.1, s32[192]{0:T(256)} %lag_hbm.1, bf16[192,128,128]{2,1,0:T(8,128)(2,1)} %k_hbm.1, bf16[6,512,128]{2,1,0:T(8,128)(2,1)} %hist_hbm.1, f32[6,128]{1,0:T(8,128)} %mk_ref.1), custom_call_target="tpu_custom_call" | custom-call | tf_op jit(solution)/shard_map/pallas_call | solution.py:380
  11.4 0.0 collective-permute-done.halo_ref
  11.4 0.0 copy-done.4
  11.5 0.0 copy-done.3
  11.5 0.0 copy-done.2
  11.5 0.0 copy-start
  11.5 1.4 %copy-done = bf16[3,512,512]{2,1,0:T(8,128)(2,1)S(1)} copy-done((bf16[3,512,512]{2,1,0:T(8,128)(2,1)S(1)}, bf16[3,512,512]{2,1,0:T(8,128)(2,1)}, u32[]{:S(2)}) %copy-start) | copy-done | bytes 1572888
  12.9 0.0 copy-start.1
  12.9 1.0 %copy-done.1 = f32[4,256,128]{2,1,0:T(8,128)S(1)} copy-done((f32[4,256,128]{2,1,0:T(8,128)S(1)}, f32[4,256,128]{2,1,0:T(8,128)}, u32[]{:S(2)}) %copy-start.1) | copy-done | bytes 524312
  13.9 38.5 %shard_map.83 = f32[4,256,128]{2,1,0:T(8,128)S(1)} custom-call(f32[4,256,128]{2,1,0:T(8,128)S(1)} %copy-done.1, bf16[3,512,512]{2,1,0:T(8,128)(2,1)S(1)} %copy-done, bf16[3,512,128]{2,1,0:T(8,128)(2,1)S(1)} %collective-permute-done.halo_ref, f32[6,128]{1,0:T(8,128)S(1)} %copy-done.4, bf16[4,256,128]{2,1,0:T(8,128)(2,1)S(1)} %copy-done.2, ...), custom_call_target="tpu_custom_call" | custom-call | tf_op jit(solution)/shard_map/pallas_call | solution.py:407
  52.4 0.8 %copy.10 = f32[4,256,128]{2,1,0:T(8,128)} copy(f32[4,256,128]{2,1,0:T(8,128)S(1)} %shard_map.83) | data formatting | bytes 1048576
Async XLA Ops:
  0.0 11.4 %copy-start.4 = (f32[6,128]{1,0:T(8,128)S(1)}, f32[6,128]{1,0:T(8,128)}, u32[]{:S(2)}) copy-start(f32[6,128]{1,0:T(8,128)} %mk_ref.1) | copy-start | bytes 9220
  0.0 11.5 %copy-start.3 = (f32[256,128]{1,0:T(8,128)S(1)}, f32[256,128]{1,0:T(8,128)}, u32[]{:S(2)}) copy-start(f32[256,128]{1,0:T(8,128)} %inv_ref.1) | copy-start | bytes 393220
  0.0 11.5 %copy-start.2 = (bf16[4,256,128]{2,1,0:T(8,128)(2,1)S(1)}, bf16[4,256,128]{2,1,0:T(8,128)(2,1)}, u32[]{:S(2)}) copy-start(bf16[4,256,128]{2,1,0:T(8,128)(2,1)} %inc_ref.1) | copy-start | bytes 786436
  1.1 10.3 %collective-permute-start = (bf16[3,512,128]{2,1,0:T(8,128)(2,1)S(1)}, bf16[3,512,128]{2,1,0:T(8,128)(2,1)S(1)}, u32[]{:S(2)}, u32[]{:S(2)}) collective-permute-start(bf16[3,512,128]{2,1,0:T(8,128)(2,1)S(1)} %slice.3), channel_id=1, source_target_pairs={{0,2},{2,4},{4,6},{6,8},{8,10},{10,12},{12,14},{14,16},{16,18},{18... | collective-permute-start | bytes 1179656 | tf_op jit(solution)/shard_map/ppermute | solution.py:378
  11.5 1.4 %copy-start = (bf16[3,512,512]{2,1,0:T(8,128)(2,1)S(1)}, bf16[3,512,512]{2,1,0:T(8,128)(2,1)}, u32[]{:S(2)}) copy-start(bf16[3,512,512]{2,1,0:T(8,128)(2,1)} %get-tuple-element.8.pair_ref) | copy-start | bytes 4718596
  12.9 1.0 %copy-start.1 = (f32[4,256,128]{2,1,0:T(8,128)S(1)}, f32[4,256,128]{2,1,0:T(8,128)}, u32[]{:S(2)}) copy-start(f32[4,256,128]{2,1,0:T(8,128)} %get-tuple-element.7.part_ref) | copy-start | bytes 1572868

commit v6 on v5

--- a/solution.py
+++ b/solution.py
@@ -244,7 +244,6 @@
             for k in range(1, n_pts):
                 copy_pts(s, k).start()
             copy7(s).start()
-            solve_pair(s)
 
     def hub_of(s):
         return jnp.where(s < BACK, 1, 0)
@@ -307,9 +306,14 @@
         pl.when(jnp.logical_and(s >= 0, s < STEPS))(lambda: act(s))
 
     def reduce_wave(t):
-        within(t, reduce_all)
+        pl.when(jnp.logical_and(jnp.logical_not(is_root), t < STEPS))(lambda: reduce_all(t))
         within(t - 1, reduce_root)
         pl.when(jnp.logical_and(is_root, t >= 2))(lambda: march(t - 2))
+
+    @pl.when(is_root)
+    def _():
+        loop(0, STEPS, reduce_all)
+        loop(0, BACK, solve_pair)
 
     loop(0, STEPS + 2, reduce_wave)
 

time: 53.4 us -> 53.5 us (level)
  no operation moved by 1% of the time
where the time goes in v6:
time: 53.5 us; the launch traced here: 53.2 us
  Pallas kernels  44.3 us (83%)
  starting transfers between devices  4.51 us (8%)
  local copies, waits for them, and re-layouts  4.33 us (8%)
    pallas_call x1, Pallas kernels, per_device(): pl.pallas_call(functools.partial(march_kernel, n, n_pts), out_shape=jax.S...  38.5 us
    pallas_call x1, Pallas kernels, per_device(): pl.pallas_call(functools.partial(history_kernel, chunks), out_shape=(jax....  5.82 us
    ppermute x1, starting transfers between devices, per_device(): lax.ppermute(history[lags - BACK:], 'lag', [(i, i + 1) for i in range(n -...  4.51 us
    unnamed x11, local copies, waits for them, and re-layouts  3.25 us
    slice x1, local copies, waits for them, and re-layouts, per_device(): history[lags - BACK:]  1.08 us
  transfers between devices with their start and end apart: 1, of which 0 were waited for; matrix products, arithmetic and copies ran while one was open for 0% of the time, Pallas kernels for 11%

profile of v6, /device:TPU:1, one launch (start us, length us, event | category | flops | bytes accessed | tf_op | source)
XLA Modules:
  0.0 53.2 jit_solution(3659722437497644913)
XLA Ops:
  0.0 0.0 copy-start.4
  0.0 0.0 copy-start.3
  0.0 0.0 copy-start.2
  0.0 1.1 %slice.3 = bf16[3,512,128]{2,1,0:T(8,128)(2,1)S(1)} slice(bf16[6,512,128]{2,1,0:T(8,128)(2,1)} %hist_hbm.1), slice={[3:6], [0:512], [0:128]} | slice | bytes 786432 | tf_op jit(solution)/shard_map/slice | solution.py:382
  1.1 4.5 %collective-permute-start = (bf16[3,512,128]{2,1,0:T(8,128)(2,1)S(1)}, bf16[3,512,128]{2,1,0:T(8,128)(2,1)S(1)}, u32[]{:S(2)}, u32[]{:S(2)}) collective-permute-start(bf16[3,512,128]{2,1,0:T(8,128)(2,1)S(1)} %slice.3), channel_id=1, source_target_pairs={{0,2},{2,4},{4,6},{6,8},{8,10},{10,12},{12,14},{14,16},{16,18},{18... | collective-permute-start | bytes 1179656 | tf_op jit(solution)/shard_map/ppermute | solution.py:382
  5.6 5.8 %shard_map.82 = (f32[4,256,128]{2,1,0:T(8,128)}, bf16[3,512,512]{2,1,0:T(8,128)(2,1)}) custom-call(s32[192]{0:T(256)} %row_hbm.1, s32[192]{0:T(256)} %col_hbm.1, s32[192]{0:T(256)} %lag_hbm.1, bf16[192,128,128]{2,1,0:T(8,128)(2,1)} %k_hbm.1, bf16[6,512,128]{2,1,0:T(8,128)(2,1)} %hist_hbm.1, f32[6,128]{1,0:T(8,128)} %mk_ref.1), custom_call_target="tpu_custom_call" | custom-call | tf_op jit(solution)/shard_map/pallas_call | solution.py:384
  11.4 0.0 collective-permute-done.halo_ref
  11.4 0.0 copy-done.4
  11.5 0.0 copy-done.3
  11.5 0.0 copy-done.2
  11.5 0.0 copy-start
  11.5 1.4 %copy-done = bf16[3,512,512]{2,1,0:T(8,128)(2,1)S(1)} copy-done((bf16[3,512,512]{2,1,0:T(8,128)(2,1)S(1)}, bf16[3,512,512]{2,1,0:T(8,128)(2,1)}, u32[]{:S(2)}) %copy-start) | copy-done | bytes 1572888
  12.9 0.0 copy-start.1
  12.9 1.0 %copy-done.1 = f32[4,256,128]{2,1,0:T(8,128)S(1)} copy-done((f32[4,256,128]{2,1,0:T(8,128)S(1)}, f32[4,256,128]{2,1,0:T(8,128)}, u32[]{:S(2)}) %copy-start.1) | copy-done | bytes 524312
  13.9 38.5 %shard_map.83 = f32[4,256,128]{2,1,0:T(8,128)S(1)} custom-call(f32[4,256,128]{2,1,0:T(8,128)S(1)} %copy-done.1, bf16[3,512,512]{2,1,0:T(8,128)(2,1)S(1)} %copy-done, bf16[3,512,128]{2,1,0:T(8,128)(2,1)S(1)} %collective-permute-done.halo_ref, f32[6,128]{1,0:T(8,128)S(1)} %copy-done.4, bf16[4,256,128]{2,1,0:T(8,128)(2,1)S(1)} %copy-done.2, ...), custom_call_target="tpu_custom_call" | custom-call | tf_op jit(solution)/shard_map/pallas_call | solution.py:411
  52.4 0.8 %copy.10 = f32[4,256,128]{2,1,0:T(8,128)} copy(f32[4,256,128]{2,1,0:T(8,128)S(1)} %shard_map.83) | data formatting | bytes 1048576
Async XLA Ops:
  0.0 11.4 %copy-start.4 = (f32[6,128]{1,0:T(8,128)S(1)}, f32[6,128]{1,0:T(8,128)}, u32[]{:S(2)}) copy-start(f32[6,128]{1,0:T(8,128)} %mk_ref.1) | copy-start | bytes 9220
  0.0 11.5 %copy-start.3 = (f32[256,128]{1,0:T(8,128)S(1)}, f32[256,128]{1,0:T(8,128)}, u32[]{:S(2)}) copy-start(f32[256,128]{1,0:T(8,128)} %inv_ref.1) | copy-start | bytes 393220
  0.0 11.5 %copy-start.2 = (bf16[4,256,128]{2,1,0:T(8,128)(2,1)S(1)}, bf16[4,256,128]{2,1,0:T(8,128)(2,1)}, u32[]{:S(2)}) copy-start(bf16[4,256,128]{2,1,0:T(8,128)(2,1)} %inc_ref.1) | copy-start | bytes 786436
  1.1 10.3 %collective-permute-start = (bf16[3,512,128]{2,1,0:T(8,128)(2,1)S(1)}, bf16[3,512,128]{2,1,0:T(8,128)(2,1)S(1)}, u32[]{:S(2)}, u32[]{:S(2)}) collective-permute-start(bf16[3,512,128]{2,1,0:T(8,128)(2,1)S(1)} %slice.3), channel_id=1, source_target_pairs={{0,2},{2,4},{4,6},{6,8},{8,10},{10,12},{12,14},{14,16},{16,18},{18... | collective-permute-start | bytes 1179656 | tf_op jit(solution)/shard_map/ppermute | solution.py:382
  11.5 1.4 %copy-start = (bf16[3,512,512]{2,1,0:T(8,128)(2,1)S(1)}, bf16[3,512,512]{2,1,0:T(8,128)(2,1)}, u32[]{:S(2)}) copy-start(bf16[3,512,512]{2,1,0:T(8,128)(2,1)} %get-tuple-element.8.pair_ref) | copy-start | bytes 4718596
  12.9 1.0 %copy-start.1 = (f32[4,256,128]{2,1,0:T(8,128)S(1)}, f32[4,256,128]{2,1,0:T(8,128)}, u32[]{:S(2)}) copy-start(f32[4,256,128]{2,1,0:T(8,128)} %get-tuple-element.7.part_ref) | copy-start | bytes 1572868
